TPU v7x, 32 devices: a whole 2x2x4 slice. The times are simulated.
32 devices in a mesh: rad: 8 (over z, y), lm: 4 (over x, core).
Axes of the slice: x: 2, y: 2, z: 4, core: 2. Of those that a mesh axis runs over, the one named last changes fastest.
Arguments:
- grid_field: bfloat16 [2, 512, 544, 128], P(None, ('rad', 'lm')), may hold values from -6 to 6
- inverses: bfloat16 [2, 64, 512, 512], P(None, ('rad', 'lm')), may hold values from -4 to 4
- slot_blocks: int32 [32, 24], replicated, may hold values from 0 to 544, as said below
- degree_start: int32 [64], replicated, may hold values from 0 to 752, as said below
Outputs:
- new_grid: bfloat16 [2, 512, 544, 128], P(None, ('rad', 'lm'))
- new_slope: bfloat16 [2, 512, 544, 128], P(None, ('rad', 'lm'))
Inputs may be any that keep to these rules, and one draw needn't show every extreme that they name: `slot_blocks`: row d lists the blocks of one degree index below 32 in order, then those of one degree index at or above it in order, then the value 544 (no block). Every block is in exactly one slot. `degree_start`: entry q equals d * 24 + s where slot s of row d of slot_blocks holds the first block of degree index q.
All inputs are finite; a program needn't handle non-finite values.
Results may differ from a plain program's by a relative error of at most 0.0052.
Values may be sent and summed in bfloat16 or wider, within the bound.
No kernel may reach another device: no remote copies, remote signals or barrier semaphores. Data moves between devices by JAX's collectives and lax.ppermute only.
A program may use at most 128 MiB of HBM per device.

v0:
```python
import functools

import jax
import jax.numpy as jnp
import numpy as np
from jax import lax
from jax.experimental import pallas as pl
from jax.experimental.pallas import tpu as pltpu
from jax.sharding import PartitionSpec as P

LMAX1 = 1024
OB = 64
AXES = ("rad", "lm")
PLANE = 8
GIFT = 8
GROUP = 16
BATCH = 34
VMEM = 48 << 20
MORE_VMEM = 60 << 20
RIDES = 16
PARTS = 4

inner_radius = 0.35
shell_depth = 0.65
diffusion_numbers = (0.9, 0.4)


def quotient(value, divisor, bound):
    numbers = np.arange(bound)
    for shift in range(24):
        factor = -(-(1 << shift) // divisor)
        if bound * factor < 2**31 and np.all(numbers * factor >> shift == numbers // divisor):
            return lax.shift_right_logical(value * factor, jnp.int32(shift))
    return lax.div(value, divisor)


class Sizes:
    def __init__(self, devices, grid_field, inverses, slot_blocks):
        self.devices = devices
        self.fields, self.local, self.blocks, self.width = grid_field.shape
        self.levels = inverses.shape[-1]
        self.capacity = slot_blocks.shape[1]
        self.degrees = 2 * devices
        self.spacing = LMAX1 // self.degrees
        self.group_size = OB * self.degrees // LMAX1
        index = np.arange(self.degrees)
        self.counts = [int(c) for c in index // self.group_size + 1]
        self.starts = [int(s) for s in np.cumsum(self.counts) - self.counts]
        self.partial = [q for q in range(self.degrees) if (q + 1) % self.group_size]

    def turns(self, q):
        return quotient(q, self.group_size, self.degrees)

    def owner(self, slot):
        return quotient(slot, self.capacity, self.devices * self.capacity)

    def last_block(self, q):
        turns = self.turns(q)
        rest = q - turns * self.group_size
        whole = lax.shift_right_logical(self.group_size * turns * (turns + 1), 1)
        return whole + rest * (turns + 1) + turns

    def last_live(self, q):
        return 2 * self.spacing * (q - self.turns(q) * self.group_size + 1)


def slot_choices(z):
    mean = -(-z.blocks // z.devices)
    return sorted({min(mean + extra, z.capacity) for extra in (0, 1, 2, 3)} | {z.capacity})


def plan_kernel(z, choices, start_ref, choice_ref, mate_ref, load_ref, high_ref, count_ref, stack_ref):
    half = z.degrees // 2
    planes = z.devices // PLANE
    kinds = z.group_size
    owner = [z.owner(start_ref[q]) for q in range(z.degrees)]
    for q in range(half, z.degrees):
        load_ref[owner[q]] = start_ref[q] - owner[q] * z.capacity + z.counts[q]
        high_ref[owner[q]] = q
    for i in range(planes * kinds):
        count_ref[i] = 0
    for q in range(z.degrees):
        mate_ref[q] = -1
    for q in z.partial:
        if q < half:
            kind = quotient(owner[q], PLANE, z.devices) * kinds + q % kinds
            stack_ref[kind * PLANE + count_ref[kind]] = q
            count_ref[kind] += 1
    for q in sorted(z.partial, key=lambda q: -(q % kinds)):
        if q < half:
            continue
        first_kind = quotient(owner[q], PLANE, z.devices) * kinds
        kind = jnp.int32(-1)
        for i in range(kinds - 1 - q % kinds):
            kind = jnp.where(count_ref[first_kind + i] > 0, first_kind + i, kind)

        @pl.when(kind >= 0)
        def _(kind=kind, q=q):
            left = count_ref[kind] - 1
            count_ref[kind] = left
            host = stack_ref[kind * PLANE + left]
            mate_ref[q] = host
            mate_ref[host] = q
            load_ref[owner[q]] -= 1

    totals = plane_totals(z, load_ref)
    most = functools.reduce(jnp.maximum, [totals[g] + totals[g + 1] for g in range(0, planes, 2)])
    highest = functools.reduce(jnp.maximum, totals)
    choice = jnp.int32(0)
    for i in range(1, len(choices)):
        tried = choices[i - 1]
        beyond = (most > 2 * PLANE * tried) | (highest > PLANE * tried + GIFT * PLANE // 2)
        choice = jnp.where(beyond, i, choice)
    choice_ref[0] = choice


def plane_totals(z, load_ref):
    return [
        sum(load_ref[g * PLANE + e] for e in range(PLANE)) for g in range(z.devices // PLANE)
    ]


def plan(z, degree_start, choices):
    smem = pl.BlockSpec(memory_space=pltpu.SMEM)
    kinds = z.devices // PLANE * z.group_size
    return pl.pallas_call(
        functools.partial(plan_kernel, z, choices),
        in_specs=[smem],
        out_specs=[smem] * 4,
        out_shape=[
            jax.ShapeDtypeStruct((size,), jnp.int32)
            for size in (1, z.degrees, z.devices, z.devices)
        ],
        scratch_shapes=[pltpu.SMEM((kinds,), jnp.int32), pltpu.SMEM((kinds * PLANE,), jnp.int32)],
        name="plan",
    )(degree_start)


def assign(z, slots, start_ref, mate_ref, load_ref, high_ref, place_ref, kept_ref, room_ref):
    totals = plane_totals(z, load_ref)
    for d in range(z.devices):
        excess = totals[d // PLANE] - PLANE * slots - GIFT * (d % PLANE // 2)
        gift = jnp.int32(0) if d % 2 else jnp.clip(excess, 0, GIFT)
        kept_ref[d] = load_ref[d] - gift
        room_ref[d ^ PLANE] = slots - gift
    for q in range(z.degrees):
        first = start_ref[q] + z.owner(start_ref[q]) * (slots - z.capacity)
        for p in range(z.counts[q]):
            place_ref[z.starts[q] + p] = first + p
    for d in range(z.devices):
        if d % PLANE == 0:
            spare = (jnp.int32(d), kept_ref[d])
        q = high_ref[d]
        last = z.last_block(q)
        first = last - z.turns(q)
        offset = start_ref[q] - d * z.capacity
        kept = kept_ref[d] - offset

        def move(state, first=first):
            p, device, slot = state
            place_ref[first + p] = device * slots + slot
            fits = slot < room_ref[device]
            after = device + 1
            return (
                jnp.where(fits, p + 1, p),
                jnp.where(fits, device, after),
                jnp.where(fits, slot + 1, kept_ref[jnp.minimum(after, z.devices - 1)]),
            )

        spare = lax.while_loop(
            lambda state, kept=kept: state[0] < kept, move, (room_ref[d] - offset, *spare)
        )[1:]
        host = mate_ref[q]
        if d % 2 == 0:
            other = d ^ PLANE
            given = other * slots + room_ref[other] - kept

            def give(p, carry, given=given, first=first):
                place_ref[first + p] = given + p
                return carry

            lax.fori_loop(kept, last - first + 1 - jnp.where(host >= 0, 1, 0), give, 0)
        start = start_ref[jnp.maximum(host, 0)]
        shared = start + z.owner(start) * (slots - z.capacity) + z.turns(host)
        place_ref[last] = jnp.where(host >= 0, shared, place_ref[last])


def swap(value, axis, bit):
    size = lax.axis_size(axis)
    return lax.ppermute(value, axis, [(i, i ^ bit) for i in range(size)])


def straight_inverses(inverses):
    own = inverses[:, 1]
    rad, lm = lax.axis_size("rad"), lax.axis_size("lm")
    facing = [(d, d ^ PLANE) for d in range(0, rad * lm, 2)]
    return own, swap(own, "lm", 2), swap(own, "rad", 1), lax.ppermute(own, AXES, facing)


def other_core(values):
    return [swap(value, "lm", 1) for value in values]


def riding(z, mate_ref, q):
    b, host = z.last_block(q), mate_ref[q]
    rides = host >= 0
    host = jnp.maximum(host, 0)
    return b, jnp.where(rides, z.last_block(host), b), jnp.where(rides, z.last_live(host), z.width)


def pack_kernel(z, f, slots, *refs):
    if f:
        place_ref, mate_ref, field_ref, out_ref, holder_ref, part_ref, wide_ref, sems = refs
    else:
        start_ref, mate_ref, load_ref, high_ref, field_ref, out_ref, place_ref = refs[:7]
        part_ref, wide_ref, sems, kept_ref, room_ref = refs[7:]
    pitch = z.blocks + 1
    some = z.local // PARTS
    copies = [
        pltpu.make_async_copy(
            field_ref.at[f, pl.ds(i * some, some)], part_ref.at[pl.ds(i * some, some)], sems.at[i]
        )
        for i in range(PARTS)
    ]
    for copy in copies:
        copy.start()
    if not f:
        assign(z, slots, start_ref, mate_ref, load_ref, high_ref, place_ref, kept_ref, room_ref)
    for level in range(z.local):
        if level % some == 0:
            copies[level // some].wait()
        wide_ref[pl.ds(level * pitch, z.blocks), :] = part_ref[level].astype(jnp.float32)

    def group(g, carry):
        for k in range(BATCH):
            b = g * BATCH + k
            tile = wide_ref[pl.ds(b, z.local, stride=pitch), :]
            out_ref[place_ref[b]] = tile.astype(jnp.bfloat16)
        return carry

    lax.fori_loop(0, z.blocks // BATCH, group, 0)
    column = lax.broadcasted_iota(jnp.int32, (z.local, z.width), 1)

    def ride(q, carry):
        b, host_block, live = riding(z, mate_ref, q)
        rider = pltpu.roll(wide_ref[pl.ds(b, z.local, stride=pitch), :], live, 1)
        tile = wide_ref[pl.ds(host_block, z.local, stride=pitch), :]
        out_ref[place_ref[b]] = jnp.where(column < live, tile, rider).astype(jnp.bfloat16)
        return carry

    lax.fori_loop(z.degrees // 2, z.degrees, ride, 0, unroll=RIDES)
    if not f:
        return

    def clear(k, carry):
        holder_ref[k] = 0
        return carry

    lax.fori_loop(0, z.devices * z.capacity, clear, 0, unroll=8)

    def degree(q, b):
        def block(p, inner):
            holder_ref[place_ref[b + p]] = q * OB + p
            return inner

        count = z.turns(q) + 1
        rides = (q >= z.degrees // 2) & (mate_ref[q] >= 0)
        lax.fori_loop(0, count - jnp.where(rides, 1, 0), block, 0)
        return b + count

    lax.fori_loop(0, z.degrees, degree, 0)


def pack(z, grid_field, f, slots, *tables):
    total = z.devices * slots
    smem = pl.BlockSpec(memory_space=pltpu.SMEM)
    table = jax.ShapeDtypeStruct((z.devices * z.capacity if f else z.blocks,), jnp.int32)
    return pl.pallas_call(
        functools.partial(pack_kernel, z, f, slots),
        in_specs=[smem] * len(tables) + [pl.BlockSpec(memory_space=pl.ANY)],
        out_specs=[pl.BlockSpec(memory_space=pltpu.VMEM), smem],
        out_shape=[jax.ShapeDtypeStruct((total, z.local, z.width), jnp.bfloat16), table],
        scratch_shapes=[
            pltpu.VMEM((z.local, z.blocks, z.width), jnp.bfloat16),
            pltpu.VMEM((z.local * (z.blocks + 1), z.width), jnp.float32),
            pltpu.SemaphoreType.DMA((PARTS,)),
        ]
        + [pltpu.SMEM((z.devices,), jnp.int32)] * (0 if f else 2),
        compiler_params=pltpu.CompilerParams(vmem_limit_bytes=VMEM),
        cost_estimate=pl.CostEstimate(flops=10**9, bytes_accessed=10**7, transcendentals=0),
        name=f"pack_{f}",
    )(*tables, grid_field)


def solve_kernel(z, f, slots, per_step, holder_ref, start_ref, mate_ref, me_ref, columns_ref, inverses_ref, *rest):
    (own, across, along, corner, own_odd, across_odd, along_odd, corner_odd, far) = rest[:9]
    out_ref, matrix_ref, square_ref, above_ref, below_ref, sems = rest[9:]
    strength = diffusion_numbers[f]
    step = pl.program_id(0)
    shape = (z.levels, z.width)
    me = me_ref[0]

    @pl.when(step == 0)
    def _():
        sources = [
            own.at[f], own_odd.at[f], across.at[f], across_odd.at[f],
            along.at[f], along_odd.at[f], corner.at[0], corner_odd.at[0],
            inverses_ref.at[f, 0], far.at[f],
        ]
        copies = [
            pltpu.make_async_copy(source, matrix_ref.at[i], sems.at[i])
            for i, source in enumerate(sources)
        ]
        for copy in copies:
            copy.start()
        level = lax.broadcasted_iota(jnp.int32, shape, 0)

        def radius(positions):
            return inner_radius + shell_depth * (positions + 1).astype(jnp.float32) / (z.levels + 1)

        here = radius(level)
        scaled = (shell_depth / (z.levels + 1)) / here
        square_ref[...] = strength * (scaled * scaled)
        above_ref[...] = jnp.where(level == z.levels - 1, 0.0, strength * radius(level + 1) / here)
        below_ref[...] = jnp.where(level == 0, 0.0, strength * radius(level - 1) / here)
        for copy in copies:
            copy.wait()

    column = lax.broadcasted_iota(jnp.int32, shape, 1)
    host = quotient(holder_ref[me * slots], OB, z.degrees * OB)
    rider = mate_ref[host]
    host_at = z.turns(host) - step * per_step
    rides = (rider >= 0) & (host_at >= 0) & (host_at < per_step)

    def block(i, carry):
        again = i >= per_step
        k = jnp.where(again, host_at, i)
        code = holder_ref[me * slots + jnp.minimum(step * per_step + k, slots - 1)]
        q = jnp.where(again, rider, quotient(code, OB, z.degrees * OB))
        value = z.spacing * (q + 1) - 1
        last = value - lax.rem(code, OB) * (z.width // 2)
        begin = jnp.where(again, z.last_live(host), 0)
        end = jnp.where(again, begin + z.last_live(rider), 2 * last + 2)
        offset = z.owner(start_ref[q]) ^ me
        which = jnp.where(offset < PLANE, offset, PLANE + 1)
        which = jnp.where(q >= z.degrees // 2, which, PLANE)
        factor = (value * (value + 1)).astype(jnp.float32)
        u = columns_ref[:, k].reshape(shape).astype(jnp.float32)
        u = jnp.where((column >= begin) & (column < end), u, 0.0)
        weight = (1.0 - 2.0 * strength) - factor * square_ref[...]
        rhs = weight * u
        rhs += above_ref[...] * pltpu.roll(u, z.levels - 1, 0)
        rhs += below_ref[...] * pltpu.roll(u, 1, 0)
        high = rhs.astype(jnp.bfloat16)
        low = (rhs - high.astype(jnp.float32)).astype(jnp.bfloat16)
        both = jnp.concatenate([high, low], axis=1)
        product = jnp.dot(matrix_ref[which], both, preferred_element_type=jnp.float32)
        solved = product[:, : z.width] + product[:, z.width :]
        earlier = out_ref[:, k].reshape(shape).astype(jnp.float32)
        solved = jnp.where(column >= begin, solved, earlier).astype(jnp.bfloat16)
        out_ref[:, k] = solved.reshape(z.devices, z.local, z.width)
        return carry

    lax.fori_loop(0, per_step + jnp.where(rides, 1, 0), block, 0)


def solve(z, holder, degree_start, mate, me, columns, inverses, pieces, f, slots):
    steps = pl.cdiv(slots, 5)
    per_step = pl.cdiv(slots, steps)
    block = (z.devices, per_step, z.local, z.width)
    spec = pl.BlockSpec(block, lambda i, *s: (0, i, 0, 0))
    return pl.pallas_call(
        functools.partial(solve_kernel, z, f, slots, per_step),
        grid_spec=pltpu.PrefetchScalarGridSpec(
            num_scalar_prefetch=4,
            grid=(steps,),
            in_specs=[spec] + [pl.BlockSpec(memory_space=pl.ANY)] * (1 + len(pieces)),
            out_specs=spec,
            scratch_shapes=[pltpu.VMEM((PLANE + 2, z.levels, z.levels), jnp.bfloat16)]
            + [pltpu.VMEM((z.levels, z.width), jnp.float32)] * 3
            + [pltpu.SemaphoreType.DMA((PLANE + 2,))],
        ),
        out_shape=jax.ShapeDtypeStruct(columns.shape, jnp.bfloat16),
        compiler_params=pltpu.CompilerParams(vmem_limit_bytes=VMEM),
        cost_estimate=pl.CostEstimate(flops=10**10, bytes_accessed=10**7, transcendentals=0),
        name=f"solve_{f}",
    )(holder, degree_start, mate, me, columns, inverses, *pieces)


def edge_slopes(z, second, before_last, before, after):
    def wide(ref):
        return ref[...].reshape(z.blocks, z.width).astype(jnp.float32)

    first = 0.5 * (wide(second) - wide(before))
    last = 0.5 * (wide(after) - wide(before_last))
    return first.astype(jnp.bfloat16), last.astype(jnp.bfloat16)


def unpack_kernel(z, f, place_ref, mate_ref, returned_ref, *rest):
    if f:
        earlier_ref, _, before_ref, after_ref, grid_ref, slope_ref, second_ref, before_last_ref = rest[:8]
        edge_ref, edge_sems = rest[-2:]
    else:
        grid_ref, slope_ref = rest[:2]
    level_ref, inner_ref, wide_ref, sems = rest[8 if f else 2 :][:4]
    pitch = z.blocks + 1
    ends = [
        pltpu.make_async_copy(
            earlier_ref.at[f - 1, level], edge_ref.at[i], edge_sems.at[i]
        )
        for i, level in enumerate((1, z.local - 2))
    ] if f else []
    for copy in ends:
        copy.start()

    def gather(g, carry):
        for k in range(BATCH):
            b = g * BATCH + k
            tile = returned_ref[place_ref[b]].astype(jnp.float32)
            wide_ref[pl.ds(b, z.local, stride=pitch), :] = tile
        return carry

    lax.fori_loop(0, z.blocks // BATCH, gather, 0)
    column = lax.broadcasted_iota(jnp.int32, (z.local, z.width), 1)

    def ride(q, carry):
        b, host_block, live = riding(z, mate_ref, q)
        tile = returned_ref[place_ref[b]].astype(jnp.float32)
        rider = pltpu.roll(tile, z.width - live, 1)
        host_rows = pl.ds(host_block, z.local, stride=pitch)
        wide_ref[host_rows, :] = jnp.where(column < live, tile, 0.0)
        rows = pl.ds(b, z.local, stride=pitch)
        wide_ref[rows, :] = jnp.where(column < z.last_live(q), rider, 0.0)
        return carry

    lax.fori_loop(z.degrees // 2, z.degrees, ride, 0, unroll=RIDES)

    def group(g, carry):
        at = pl.multiple_of(g * GROUP, GROUP)
        rows = pl.ds(at, GROUP)
        value = [wide_ref[pl.ds(at + i * pitch, GROUP), :] for i in range(z.local)]
        for i in range(z.local):
            level_ref[i, rows, :] = value[i].astype(jnp.bfloat16)
        for i in range(1, z.local - 1):
            slope = 0.5 * (value[i + 1] - value[i - 1])
            inner_ref[i - 1, rows, :] = slope.astype(jnp.bfloat16)
        if f:
            second_ref[rows, :] = value[1].astype(jnp.bfloat16)
            before_last_ref[rows, :] = value[-2].astype(jnp.bfloat16)
        return carry

    groups = z.blocks // GROUP
    copies = []
    for i in range(PARTS):
        begin, end = i * groups // PARTS, (i + 1) * groups // PARTS
        lax.fori_loop(begin, end, group, 0)
        rows = pl.ds(begin * GROUP, (end - begin) * GROUP)
        copies += [
            pltpu.make_async_copy(
                level_ref.at[:, rows, :], grid_ref.at[f, :, rows, :], sems.at[2 * i]
            ),
            pltpu.make_async_copy(
                inner_ref.at[:, rows, :],
                slope_ref.at[f, pl.ds(1, z.local - 2), rows, :],
                sems.at[2 * i + 1],
            ),
        ]
        for copy in copies[-2:]:
            copy.start()
    if f:
        for copy in ends:
            copy.wait()
        slopes = edge_slopes(z, edge_ref.at[0], edge_ref.at[1], before_ref, after_ref)
        for i, level in enumerate((0, z.local - 1)):
            edge_ref[2 + i] = slopes[i]
            copy = pltpu.make_async_copy(
                edge_ref.at[2 + i], slope_ref.at[f - 1, level], edge_sems.at[2 + i]
            )
            copy.start()
            copies.append(copy)
    for copy in copies:
        copy.wait()


def unpack(z, place, mate, returned, f, earlier):
    whole = jax.ShapeDtypeStruct((z.fields, z.local, z.blocks, z.width), jnp.bfloat16)
    level = jax.ShapeDtypeStruct((z.blocks, z.width), jnp.bfloat16)
    smem, anywhere = pl.BlockSpec(memory_space=pltpu.SMEM), pl.BlockSpec(memory_space=pl.ANY)
    vmem = pl.BlockSpec(memory_space=pltpu.VMEM)
    edge_scratch = [
        pltpu.VMEM((4, z.blocks, z.width), jnp.bfloat16),
        pltpu.SemaphoreType.DMA((4,)),
    ]
    return pl.pallas_call(
        functools.partial(unpack_kernel, z, f),
        in_specs=[smem, smem, vmem] + [anywhere, anywhere, vmem, vmem] * min(f, 1),
        out_specs=[anywhere] * 2 + [vmem] * 2 * min(f, 1),
        out_shape=[whole] * 2 + [level] * 2 * min(f, 1),
        scratch_shapes=[
            pltpu.VMEM((z.local, z.blocks, z.width), jnp.bfloat16),
            pltpu.VMEM((z.local - 2, z.blocks, z.width), jnp.bfloat16),
            pltpu.VMEM((z.local * (z.blocks + 1), z.width), jnp.float32),
            pltpu.SemaphoreType.DMA((2 * PARTS,)),
        ]
        + edge_scratch * min(f, 1),
        input_output_aliases={3: 0, 4: 1} if f else {},
        compiler_params=pltpu.CompilerParams(vmem_limit_bytes=VMEM if f else MORE_VMEM),
        cost_estimate=pl.CostEstimate(flops=10**9, bytes_accessed=10**7, transcendentals=0),
        name=f"unpack_{f}",
    )(place, mate, returned, *earlier)


def rim_kernel(z, place_ref, mate_ref, returned_ref, first_ref, last_ref, first_wide_ref, last_wide_ref):
    sides = ((first_wide_ref, 0), (last_wide_ref, z.local - 1))

    def gather(g, carry):
        for k in range(BATCH):
            b = g * BATCH + k
            tile = returned_ref[place_ref[b]].astype(jnp.float32)
            for wide_ref, row in sides:
                wide_ref[pl.ds(b, 1), :] = tile[row : row + 1]
        return carry

    lax.fori_loop(0, z.blocks // BATCH, gather, 0)
    column = lax.broadcasted_iota(jnp.int32, (z.local, z.width), 1)

    def ride(q, carry):
        b, host_block, live = riding(z, mate_ref, q)
        tile = returned_ref[place_ref[b]].astype(jnp.float32)
        rider = pltpu.roll(tile, z.width - live, 1)
        rider = jnp.where(column < z.last_live(q), rider, 0.0)
        tile = jnp.where(column < live, tile, 0.0)
        for wide_ref, row in sides:
            wide_ref[pl.ds(host_block, 1), :] = tile[row : row + 1]
            wide_ref[pl.ds(b, 1), :] = rider[row : row + 1]
        return carry

    lax.fori_loop(z.degrees // 2, z.degrees, ride, 0, unroll=RIDES)
    first_ref[0] = first_wide_ref[...].astype(jnp.bfloat16)
    last_ref[0] = last_wide_ref[...].astype(jnp.bfloat16)


def rims(z, place, mate, returned, f):
    level = jax.ShapeDtypeStruct((1, z.blocks, z.width), jnp.bfloat16)
    spec = pl.BlockSpec(level.shape, lambda i, *s: (0, 0, 0))
    return pl.pallas_call(
        functools.partial(rim_kernel, z),
        grid_spec=pltpu.PrefetchScalarGridSpec(
            num_scalar_prefetch=2,
            grid=(1,),
            in_specs=[pl.BlockSpec(returned.shape, lambda i, *s: (0, 0, 0))],
            out_specs=[spec, spec],
            scratch_shapes=[pltpu.VMEM((z.blocks, z.width), jnp.float32)] * 2,
        ),
        out_shape=[level, level],
        compiler_params=pltpu.CompilerParams(vmem_limit_bytes=VMEM if f else MORE_VMEM),
        cost_estimate=pl.CostEstimate(flops=10**8, bytes_accessed=3 * 10**6, transcendentals=0),
        name=f"rims_{f}",
    )(place, mate, returned)


def edge_kernel(z, f, second_ref, before_last_ref, before_ref, after_ref, _, slope_ref, edge_ref, sems):
    slopes = edge_slopes(z, second_ref, before_last_ref, before_ref, after_ref)
    copies = []
    for i, level in enumerate((0, z.local - 1)):
        edge_ref[i] = slopes[i]
        copies.append(pltpu.make_async_copy(edge_ref.at[i], slope_ref.at[f, level], sems.at[i]))
        copies[i].start()
    for copy in copies:
        copy.wait()


def edges(z, slope, inside, outside, f):
    vmem, anywhere = pl.BlockSpec(memory_space=pltpu.VMEM), pl.BlockSpec(memory_space=pl.ANY)
    return pl.pallas_call(
        functools.partial(edge_kernel, z, f),
        in_specs=[vmem] * 4 + [anywhere],
        out_specs=anywhere,
        out_shape=jax.ShapeDtypeStruct(slope.shape, slope.dtype),
        scratch_shapes=[
            pltpu.VMEM((2, z.blocks, z.width), jnp.bfloat16),
            pltpu.SemaphoreType.DMA((2,)),
        ],
        input_output_aliases={4: 0},
        compiler_params=pltpu.CompilerParams(vmem_limit_bytes=VMEM),
        name=f"edges_{f}",
    )(*inside, *outside, slope)


def beside(z, first, last):
    up = [(i, i + 1) for i in range(z.devices - 1)]
    down = [(j, i) for i, j in up]
    return lax.ppermute(last, AXES, up), lax.ppermute(first, AXES, down)


def exchange(z, value, slots):
    shaped = value.reshape(z.devices, slots, z.local, z.width)
    return lax.all_to_all(shaped, AXES, split_axis=0, concat_axis=0, tiled=True)


def body(grid_field, inverses, slot_blocks, degree_start):
    rad, lm = lax.axis_size("rad"), lax.axis_size("lm")
    z = Sizes(rad * lm, grid_field, inverses, slot_blocks)
    choices = slot_choices(z)
    kernels = z.local % 16 == 0 and z.fields == 2 and z.blocks % GROUP == 0 and rad % 4 == 0 and lm == PLANE // 2
    low, high = z.counts[z.degrees // 2 - 1 : z.degrees // 2 + 1]
    if not kernels or low + GIFT > choices[0] or high <= GIFT or z.capacity - choices[0] > GIFT:
        return plain_body(z, grid_field, inverses, degree_start)
    me = lax.axis_index(AXES).reshape(1).astype(jnp.int32)
    choice, *tables = plan(z, degree_start, choices)
    routes = [functools.partial(route, z, slots) for slots in choices]
    return lax.switch(choice[0], routes, grid_field, inverses, degree_start, me, *tables)


def route(z, slots, grid_field, inverses, degree_start, me, mate, load, high):
    sent_0, place = pack(z, grid_field, 0, slots, degree_start, mate, load, high)
    sent_1, holder = pack(z, grid_field, 1, slots, place, mate)
    sent_1, own, across, along, far = lax.optimization_barrier(
        (sent_1, *straight_inverses(inverses))
    )
    columns = [exchange(z, sent, slots) for sent in (sent_0, sent_1)]
    corner_0 = swap(across[:1], "rad", 1)
    even = [own, across, along]
    odd = other_core(even)
    pieces = lax.optimization_barrier((*even, corner_0, *odd, *other_core([corner_0]), far))
    solved_0 = solve(z, holder, degree_start, mate, me, columns[0], inverses, pieces, 0, slots)
    corner_1 = swap(along[1:], "lm", 2)
    pieces = (*even, corner_1, *odd, *other_core([corner_1]), far)
    solved_1 = solve(z, holder, degree_start, mate, me, columns[1], inverses, pieces, 1, slots)
    solved = [solved_0, solved_1]
    returned = [
        exchange(z, solved[f], slots).reshape(z.devices * slots, z.local, z.width)
        for f in range(z.fields)
    ]
    outside = beside(z, *rims(z, place, mate, returned[0], 0))
    outs = unpack(z, place, mate, returned[0], 0, ())
    last, *outs = lax.optimization_barrier((returned[1], *outs))
    last_outside = beside(z, *rims(z, place, mate, last, 1))
    grid, slope, *inside = unpack(z, place, mate, last, 1, (*outs, *outside))
    return grid, edges(z, slope, inside, last_outside, 1)


def plain_body(z, grid_field, inverses, degree_start):
    index = np.arange(z.degrees)
    counts = np.asarray(z.counts)
    degree_of = np.repeat(index, counts)
    place_in = np.arange(z.blocks) - np.asarray(z.starts)[degree_of]
    value = z.spacing * (index + 1) - 1
    slot_place = degree_start[degree_of] + jnp.asarray(place_in, jnp.int32)
    total = z.devices * z.capacity
    holder = jnp.full((total,), z.blocks, jnp.int32)
    holder = holder.at[slot_place].set(jnp.arange(z.blocks, dtype=jnp.int32))
    sent = jnp.take(grid_field, holder, axis=2, mode="fill", fill_value=0)
    sent = sent.reshape(z.fields, z.local, z.devices, z.capacity, z.width)
    columns = lax.all_to_all(sent, AXES, split_axis=2, concat_axis=1, tiled=True)
    columns = columns.reshape(z.fields, z.levels, z.capacity, z.width)
    device = lax.axis_index(AXES)
    mine = lax.dynamic_slice_in_dim(holder, device * z.capacity, z.capacity)
    order = jnp.asarray(place_in)[:, None] * OB + np.arange(z.width)[None, :] // 2
    live_table = (order <= jnp.asarray(value[degree_of])[:, None]).astype(jnp.float32)
    live = jnp.take(live_table, mine, axis=0, mode="fill", fill_value=0)
    factor = (value * (value + 1)).astype(np.float32)[degree_of]
    factor = jnp.take(jnp.asarray(factor), mine, mode="fill", fill_value=0)
    upper = jnp.take(jnp.asarray(degree_of >= z.degrees // 2), mine, mode="fill", fill_value=False)
    radius = inner_radius + shell_depth * jnp.arange(z.levels + 2, dtype=jnp.float32) / (z.levels + 1)
    here = radius[1:-1][None, :, None, None]
    padded = jnp.pad(columns.astype(jnp.float32), ((0, 0), (1, 1), (0, 0), (0, 0)))
    weighted = padded * radius[None, :, None, None]
    second = (weighted[:, 2:] - 2.0 * weighted[:, 1:-1] + weighted[:, :-2]) / here
    scaled = (shell_depth / (z.levels + 1)) / here
    centre = padded[:, 1:-1]
    strength = jnp.asarray(diffusion_numbers, jnp.float32)[:, None, None, None]
    angular = factor[None, None, :, None] * (scaled * scaled) * centre
    rhs = (centre + strength * (second - angular)) * live[None, None]

    def solve_slot(carry, at):
        matrix = lax.dynamic_index_in_dim(
            inverses, upper[at].astype(jnp.int32), 1, keepdims=False
        ).astype(jnp.float32)
        block = lax.dynamic_index_in_dim(rhs, at, 2, keepdims=False)
        product = jnp.einsum("fij,fjc->fic", matrix, block, precision=lax.Precision.HIGHEST)
        return carry, product.astype(jnp.bfloat16)

    solved = lax.scan(solve_slot, 0, jnp.arange(z.capacity))[1]
    solved = jnp.moveaxis(solved, 0, 2)
    solved = solved.reshape(z.fields, z.devices, z.local, z.capacity, z.width)
    returned = lax.all_to_all(solved, AXES, split_axis=1, concat_axis=3, tiled=True)
    returned = returned.reshape(z.fields, z.local, total, z.width)
    grid = jnp.take(returned, slot_place, axis=2)
    before, after = beside(z, grid[:, :1], grid[:, -1:])
    rimmed = jnp.concatenate([before, grid, after], axis=1).astype(jnp.float32)
    return grid, (0.5 * (rimmed[:, 2:] - rimmed[:, :-2])).astype(jnp.bfloat16)


def solution(mesh):
    in_specs = (P(None, AXES), P(None, AXES), P(), P())
    out_specs = (P(None, AXES), P(None, AXES))
    return jax.shard_map(body, mesh=mesh, in_specs=in_specs, out_specs=out_specs, check_vma=False)
```

profile of v0, /device:TPU:15, one launch (start us, length us, event | category | flops | bytes accessed | tf_op | source)
XLA Modules:
  0.0 256.9 jit_solution(12719860058974890667)
XLA Ops:
  0.6 1.9 plan.1
  3.2 253.5 %conditional.1 = (bf16[2,16,544,128]{3,2,1,0:T(8,128)(2,1)}, bf16[2,16,544,128]{3,2,1,0:T(8,128)(2,1)}) conditional(s32[]{:T(128)} %bitcast.30, (s32[64]{0:T(128)}, s32[64]{0:T(128)S(1)}, s32[32]{0:T(128)S(1)}, s32[32]{0:T(128)S(1)}, bf16[2,16,544,128]{3,2,1,0:T(8,128)(2,1)}, ...), branch_computations={%region_0.0_spmd, %region_1.0_spmd, %region_2.0_spmd, %region_3.0_... | conditional | flops 24199999488 | bytes 156327888 | solution.py:612
  3.2 4.9 %pack_0.6 = (bf16[576,16,128]{2,1,0:T(8,128)(2,1)}, s32[544]{0:T(1024)S(1)}) custom-call(s32[64]{0:T(128)} %get-tuple-element.108.refs_0_.start_ref, s32[64]{0:T(128)S(1)} %get-tuple-element.109.refs_1_.mate_ref, s32[32]{0:T(128)S(1)} %get-tuple-element.110.refs_2_, s32[32]{0:T(128)S(1)} %get-tuple-element.111.refs_3_, ...), custom_call_target="tpu_custom_call" | custom-call | flops 1000000000 | bytes 10000000 | tf_op jit(solution)/shard_map/cond/branch_1_fun/pack_0/pallas_call | solution.py:278
  8.1 0.0 copy-start.11
  8.1 6.3 %all-to-all-start.6 = ((bf16[32,18,16,128]{3,2,1,0:T(8,128)(2,1)}), bf16[32,18,16,128]{3,2,1,0:T(8,128)(2,1)}, u32[]{:S(2)}, u32[]{:S(2)}) async-start(bf16[32,18,16,128]{3,2,1,0:T(8,128)(2,1)} %bitcast.10), calls=%async_computation.6 | async-start | bytes 4718592 | tf_op jit(solution)/shard_map/cond/branch_1_fun/all_to_all | solution.py:598
  14.4 0.1 slice_bitcast_fusion.1.rest_0_
  14.5 0.7 collective-permute-start.16
  15.3 0.3 collective-permute-start.15
  15.6 0.3 collective-permute-start.14
  15.9 9.8 %pack_1.6 = (bf16[576,16,128]{2,1,0:T(8,128)(2,1)}, s32[768]{0:T(1024)S(1)}) custom-call(s32[544]{0:T(1024)S(1)} %get-tuple-element.113.refs_0_.place_ref, s32[64]{0:T(128)S(1)} %get-tuple-element.109.refs_1_.mate_ref, bf16[2,16,544,128]{3,2,1,0:T(8,128)(2,1)} %get-tuple-element.287.refs_4_.refs_2_), custom_call_target="tpu_custom_call" | custom-call | flops 1000000000 | bytes 10000000 | tf_op jit(solution)/shard_map/cond/branch_1_fun/pack_1/pallas_call | solution.py:278
  25.7 0.0 collective-permute-done.16.rest_8_
  25.7 38.1 %collective-permute-done.15.rest_2_ = bf16[2,512,512]{2,1,0:T(8,128)(2,1)S(1)} collective-permute-done((bf16[2,512,512]{2,1,0:T(8,128)(2,1)S(1)}, bf16[2,512,512]{2,1,0:T(8,128)(2,1)S(1)}, u32[]{:S(2)}, u32[]{:S(2)}) %collective-permute-start.15) | collective-permute-done | bytes 1048608 | tf_op jit(solution)/shard_map/cond/branch_1_fun/ppermute | solution.py:190
  63.8 0.0 collective-permute-done.14.rest_1_
  63.8 2.6 all-to-all-done.6.columns_ref
  66.4 6.9 %all-to-all-start.4 = ((bf16[32,18,16,128]{3,2,1,0:T(8,128)(2,1)}), bf16[32,18,16,128]{3,2,1,0:T(8,128)(2,1)}, u32[]{:S(2)}, u32[]{:S(2)}) async-start(bf16[32,18,16,128]{3,2,1,0:T(8,128)(2,1)} %bitcast.8), calls=%async_computation.4 | async-start | bytes 4718592 | tf_op jit(solution)/shard_map/cond/branch_1_fun/all_to_all | solution.py:598
  73.3 0.3 collective-permute-start.22
  73.7 0.6 collective-permute-start.19
  74.3 0.0 collective-permute-start.18
  74.3 0.5 collective-permute-start.20
  74.8 32.6 %collective-permute-done.22.rest_3_ = bf16[1,512,512]{2,1,0:T(8,128)(2,1)} collective-permute-done((bf16[1,512,512]{2,1,0:T(8,128)(2,1)S(1)}, bf16[1,512,512]{2,1,0:T(8,128)(2,1)}, u32[]{:S(2)}, u32[]{:S(2)}) %collective-permute-start.22) | collective-permute-done | bytes 524320 | tf_op jit(solution)/shard_map/cond/branch_1_fun/ppermute | solution.py:190
  107.5 0.4 collective-permute-start.23
  107.9 1.9 collective-permute-done.23.rest_7_
  109.8 0.0 collective-permute-done.18.rest_4_
  109.8 0.0 collective-permute-done.19.rest_5_
  109.8 0.0 collective-permute-done.20.rest_6_
  109.8 13.5 %solve_0.6 = bf16[32,18,16,128]{3,2,1,0:T(8,128)(2,1)} custom-call(s32[768]{0:T(1024)S(1)} %get-tuple-element.114.holder_ref, s32[64]{0:T(128)S(1)} %copy-done.16, s32[64]{0:T(128)S(1)} %get-tuple-element.109.refs_1_.mate_ref, s32[1]{0:T(128)} %bitcast.6.me_ref, bf16[32,18,16,128]{3,2,1,0:T(8,128)(2,1)} %all-to-all-done.6.columns_ref, ...), custom_call_target="tpu_custom_call" | custom-call | flops 10000000000 | bytes 10000000 | tf_op jit(solution)/shard_map/cond/branch_1_fun/solve_0/pallas_call | solution.py:372
  123.4 1.7 all-to-all-done.4.columns_ref
  125.0 6.9 %all-to-all-start.7 = ((bf16[32,18,16,128]{3,2,1,0:T(8,128)(2,1)}), bf16[32,18,16,128]{3,2,1,0:T(8,128)(2,1)}, u32[]{:S(2)}, u32[]{:S(2)}) async-start(bf16[32,18,16,128]{3,2,1,0:T(8,128)(2,1)} %solve_0.6), calls=%async_computation.7 | async-start | bytes 4718592 | tf_op jit(solution)/shard_map/cond/branch_1_fun/all_to_all | solution.py:598
  132.0 0.3 collective-permute-start.17
  132.3 32.3 %collective-permute-done.17.rest_3_ = bf16[1,512,512]{2,1,0:T(8,128)(2,1)S(1)} collective-permute-done((bf16[1,512,512]{2,1,0:T(8,128)(2,1)S(1)}, bf16[1,512,512]{2,1,0:T(8,128)(2,1)S(1)}, u32[]{:S(2)}, u32[]{:S(2)}) %collective-permute-start.17) | collective-permute-done | bytes 524320 | tf_op jit(solution)/shard_map/cond/branch_1_fun/ppermute | solution.py:190
  164.6 2.3 collective-permute-start.21
  166.9 1.5 collective-permute-done.21.rest_7_
  168.4 13.3 %solve_1.6 = bf16[32,18,16,128]{3,2,1,0:T(8,128)(2,1)} custom-call(s32[768]{0:T(1024)S(1)} %get-tuple-element.114.holder_ref, s32[64]{0:T(128)S(1)} %copy-done.16, s32[64]{0:T(128)S(1)} %get-tuple-element.109.refs_1_.mate_ref, s32[1]{0:T(128)} %bitcast.6.me_ref, bf16[32,18,16,128]{3,2,1,0:T(8,128)(2,1)} %all-to-all-done.4.columns_ref, ...), custom_call_target="tpu_custom_call" | custom-call | flops 10000000000 | bytes 10000000 | tf_op jit(solution)/shard_map/cond/branch_1_fun/solve_1/pallas_call | solution.py:372
  181.7 2.0 all-to-all-done.7
  183.7 6.8 %all-to-all-start.5 = ((bf16[32,18,16,128]{3,2,1,0:T(8,128)(2,1)}), bf16[32,18,16,128]{3,2,1,0:T(8,128)(2,1)S(1)}, u32[]{:S(2)}, u32[]{:S(2)}) async-start(bf16[32,18,16,128]{3,2,1,0:T(8,128)(2,1)} %solve_1.6), calls=%async_computation.5 | async-start | bytes 4718592 | tf_op jit(solution)/shard_map/cond/branch_1_fun/all_to_all | solution.py:598
  190.5 4.3 %rims_0.6 = (bf16[1,544,128]{2,1,0:T(8,128)(2,1)}, bf16[1,544,128]{2,1,0:T(8,128)(2,1)}) custom-call(s32[544]{0:T(1024)} %copy-done.8, s32[64]{0:T(128)S(1)} %get-tuple-element.109.refs_1_.mate_ref, bf16[576,16,128]{2,1,0:T(8,128)(2,1)} %bitcast.11.returned_ref), custom_call_target="tpu_custom_call" | custom-call | flops 100000000 | bytes 3000000 | tf_op jit(solution)/shard_map/cond/branch_1_fun/rims_0/pallas_call | solution.py:546
  194.9 3.3 %collective-permute-start.24 = (bf16[1,544,128]{2,1,0:T(8,128)(2,1)}, bf16[1,544,128]{2,1,0:T(8,128)(2,1)S(1)}, u32[]{:S(2)}, u32[]{:S(2)}) collective-permute-start(bf16[1,544,128]{2,1,0:T(8,128)(2,1)} %get-tuple-element.138), channel_id=1, source_target_pairs={{0,1},{1,2},{2,3},{3,4},{4,5},{5,6},{6,7},{7,8},{8,9},{9,10},{10,1... | collective-permute-start | bytes 417800 | tf_op jit(solution)/shard_map/cond/branch_1_fun/ppermute | solution.py:593
  198.2 1.9 collective-permute-start.25
  200.1 5.0 %unpack_0.6 = (bf16[2,16,544,128]{3,2,1,0:T(8,128)(2,1)}, bf16[2,16,544,128]{3,2,1,0:T(8,128)(2,1)}) custom-call(s32[544]{0:T(1024)} %copy-done.8, s32[64]{0:T(128)S(1)} %get-tuple-element.109.refs_1_.mate_ref, bf16[576,16,128]{2,1,0:T(8,128)(2,1)} %bitcast.11.returned_ref), custom_call_target="tpu_custom_call" | custom-call | flops 1000000000 | bytes 10000000 | tf_op jit(solution)/shard_map/cond/branch_1_fun/unpack_0/pallas_call | solution.py:494
  205.2 37.2 %all-to-all-done.5 = bf16[32,18,16,128]{3,2,1,0:T(8,128)(2,1)S(1)} async-done(((bf16[32,18,16,128]{3,2,1,0:T(8,128)(2,1)}), bf16[32,18,16,128]{3,2,1,0:T(8,128)(2,1)S(1)}, u32[]{:S(2)}, u32[]{:S(2)}) %all-to-all-start.5) | async-done | bytes 2359328 | tf_op jit(solution)/shard_map/cond/branch_1_fun/all_to_all | solution.py:598
  242.3 1.7 rims_1.6
  244.1 3.1 %collective-permute-start.26 = (bf16[1,544,128]{2,1,0:T(8,128)(2,1)S(1)}, bf16[1,544,128]{2,1,0:T(8,128)(2,1)S(1)}, u32[]{:S(2)}, u32[]{:S(2)}) collective-permute-start(bf16[1,544,128]{2,1,0:T(8,128)(2,1)S(1)} %get-tuple-element.143), channel_id=1, source_target_pairs={{0,1},{1,2},{2,3},{3,4},{4,5},{5,6},{6,7},{7,8},{8,9},{9,10},{10,1... | collective-permute-start | bytes 417800 | tf_op jit(solution)/shard_map/cond/branch_1_fun/ppermute | solution.py:593
  247.2 1.9 collective-permute-start.27
  249.1 0.0 collective-permute-done.24.rest_2_
  249.1 0.0 collective-permute-done.25.rest_3_
  249.1 4.0 %unpack_1.6 = (bf16[2,16,544,128]{3,2,1,0:T(8,128)(2,1)}, bf16[2,16,544,128]{3,2,1,0:T(8,128)(2,1)}, bf16[544,128]{1,0:T(8,128)(2,1)S(1)}, bf16[544,128]{1,0:T(8,128)(2,1)S(1)}) custom-call(s32[544]{0:T(1024)S(1)} %copy-done.9, s32[64]{0:T(128)S(1)} %get-tuple-element.109.refs_1_.mate_ref, ...), custom_call_target="tpu_custom_call", output_to_operand_aliasing={{0}: (3, {}), {1}: (4, {})} | custom-call | flops 1000000000 | bytes 10000000 | tf_op jit(solution)/shard_map/cond/branch_1_fun/unpack_1/pallas_call | solution.py:494
  253.2 2.2 collective-permute-done.27.after_ref
  255.3 0.8 edges_1.6
  (12 shorter events, 0.1 us)
Async XLA Ops:
  8.1 7.8 %copy-start.8 = (s32[544]{0:T(1024)}, s32[544]{0:T(1024)S(1)}, u32[]{:S(2)}) copy-start(s32[544]{0:T(1024)S(1)} %get-tuple-element.113.refs_0_.place_ref) | copy-start | bytes 6532 | tf_op jit(solution)/shard_map/cond
  8.1 6.4 %copy-start.11 = (bf16[2,2,512,512]{3,2,1,0:T(8,128)(2,1)S(1)}, bf16[2,2,512,512]{3,2,1,0:T(8,128)(2,1)}, u32[]{:S(2)}) copy-start(bf16[2,2,512,512]{3,2,1,0:T(8,128)(2,1)} %get-tuple-element.330.inverses_ref) | copy-start | bytes 6291460 | tf_op jit(solution)/shard_map/cond
  8.1 58.3 %all-to-all-start.6 = ((bf16[32,18,16,128]{3,2,1,0:T(8,128)(2,1)}), bf16[32,18,16,128]{3,2,1,0:T(8,128)(2,1)}, u32[]{:S(2)}, u32[]{:S(2)}) async-start(bf16[32,18,16,128]{3,2,1,0:T(8,128)(2,1)} %bitcast.10), calls=%async_computation.6 | async-start | bytes 4718592 | tf_op jit(solution)/shard_map/cond/branch_1_fun/all_to_all | solution.py:598
  14.5 11.1 %collective-permute-start.16 = (bf16[2,512,512]{2,1,0:T(8,128)(2,1)S(1)}, bf16[2,512,512]{2,1,0:T(8,128)(2,1)S(1)}, u32[]{:S(2)}, u32[]{:S(2)}) collective-permute-start(bf16[2,512,512]{2,1,0:T(8,128)(2,1)S(1)} %slice_bitcast_fusion.1.rest_0_), channel_id=1, source_target_pairs={{0,8},{2,10},{4,12},{6,14},{8,0},{10,2},{12,4},{14,6},{16,24},{18,... | collective-permute-start | bytes 3145736 | tf_op jit(solution)/shard_map/cond/branch_1_fun/ppermute | solution.py:197
  15.3 48.6 %collective-permute-start.15 = (bf16[2,512,512]{2,1,0:T(8,128)(2,1)S(1)}, bf16[2,512,512]{2,1,0:T(8,128)(2,1)S(1)}, u32[]{:S(2)}, u32[]{:S(2)}) collective-permute-start(bf16[2,512,512]{2,1,0:T(8,128)(2,1)S(1)} %slice_bitcast_fusion.1.rest_0_), channel_id=1, source_target_pairs={{0,4},{4,0},{8,12},{12,8},{16,20},{20,16},{24,28},{28,24},{1,5},{5... | collective-permute-start | bytes 3145736 | tf_op jit(solution)/shard_map/cond/branch_1_fun/ppermute | solution.py:190
  15.6 48.2 %collective-permute-start.14 = (bf16[2,512,512]{2,1,0:T(8,128)(2,1)S(1)}, bf16[2,512,512]{2,1,0:T(8,128)(2,1)S(1)}, u32[]{:S(2)}, u32[]{:S(2)}) collective-permute-start(bf16[2,512,512]{2,1,0:T(8,128)(2,1)S(1)} %slice_bitcast_fusion.1.rest_0_), channel_id=1, source_target_pairs={{0,2},{1,3},{2,0},{3,1},{4,6},{5,7},{6,4},{7,5},{8,10},{9,11},{10,... | collective-permute-start | bytes 3145736 | tf_op jit(solution)/shard_map/cond/branch_1_fun/ppermute | solution.py:190
  25.7 38.1 %copy-start.21 = (bf16[2,512,512]{2,1,0:T(8,128)(2,1)}, bf16[2,512,512]{2,1,0:T(8,128)(2,1)S(1)}, u32[]{:S(2)}) copy-start(bf16[2,512,512]{2,1,0:T(8,128)(2,1)S(1)} %collective-permute-done.16.rest_8_) | copy-start | bytes 3145732 | tf_op jit(solution)/shard_map/cond
  66.4 43.4 %copy-start.16 = (s32[64]{0:T(128)S(1)}, s32[64]{0:T(128)}, u32[]{:S(2)}) copy-start(s32[64]{0:T(128)} %get-tuple-element.108.refs_0_.start_ref) | copy-start | bytes 772 | tf_op jit(solution)/shard_map/cond
  66.4 58.7 %all-to-all-start.4 = ((bf16[32,18,16,128]{3,2,1,0:T(8,128)(2,1)}), bf16[32,18,16,128]{3,2,1,0:T(8,128)(2,1)}, u32[]{:S(2)}, u32[]{:S(2)}) async-start(bf16[32,18,16,128]{3,2,1,0:T(8,128)(2,1)} %bitcast.8), calls=%async_computation.4 | async-start | bytes 4718592 | tf_op jit(solution)/shard_map/cond/branch_1_fun/all_to_all | solution.py:598
  73.3 34.1 %collective-permute-start.22 = (bf16[1,512,512]{2,1,0:T(8,128)(2,1)S(1)}, bf16[1,512,512]{2,1,0:T(8,128)(2,1)}, u32[]{:S(2)}, u32[]{:S(2)}) collective-permute-start(bf16[1,512,512]{2,1,0:T(8,128)(2,1)S(1)} %slice.35), channel_id=1, source_target_pairs={{0,4},{4,0},{8,12},{12,8},{16,20},{20,16},{24,28},{28,24},{1,5},{5... | collective-permute-start | bytes 1572872 | tf_op jit(solution)/shard_map/cond/branch_1_fun/ppermute | solution.py:190
  73.7 36.1 %collective-permute-start.19 = (bf16[2,512,512]{2,1,0:T(8,128)(2,1)S(1)}, bf16[2,512,512]{2,1,0:T(8,128)(2,1)}, u32[]{:S(2)}, u32[]{:S(2)}) collective-permute-start(bf16[2,512,512]{2,1,0:T(8,128)(2,1)S(1)} %collective-permute-done.14.rest_1_), channel_id=1, source_target_pairs={{0,1},{1,0},{2,3},{3,2},{4,5},{5,4},{6,7},{7,6},{8,9},{9,8},{10,11... | collective-permute-start | bytes 3145736 | tf_op jit(solution)/shard_map/cond/branch_1_fun/ppermute | solution.py:190
  74.3 35.5 %collective-permute-start.18 = (bf16[2,512,512]{2,1,0:T(8,128)(2,1)S(1)}, bf16[2,512,512]{2,1,0:T(8,128)(2,1)}, u32[]{:S(2)}, u32[]{:S(2)}) collective-permute-start(bf16[2,512,512]{2,1,0:T(8,128)(2,1)S(1)} %slice_bitcast_fusion.1.rest_0_), channel_id=1, source_target_pairs={{0,1},{1,0},{2,3},{3,2},{4,5},{5,4},{6,7},{7,6},{8,9},{9,8},{10,11... | collective-permute-start | bytes 3145736 | tf_op jit(solution)/shard_map/cond/branch_1_fun/ppermute | solution.py:190
  74.3 35.5 %collective-permute-start.20 = (bf16[2,512,512]{2,1,0:T(8,128)(2,1)S(1)}, bf16[2,512,512]{2,1,0:T(8,128)(2,1)}, u32[]{:S(2)}, u32[]{:S(2)}) collective-permute-start(bf16[2,512,512]{2,1,0:T(8,128)(2,1)S(1)} %collective-permute-done.15.rest_2_), channel_id=1, source_target_pairs={{0,1},{1,0},{2,3},{3,2},{4,5},{5,4},{6,7},{7,6},{8,9},{9,8},{10,11... | collective-permute-start | bytes 3145736 | tf_op jit(solution)/shard_map/cond/branch_1_fun/ppermute | solution.py:190
  107.5 2.3 collective-permute-start.23
  125.0 58.7 %all-to-all-start.7 = ((bf16[32,18,16,128]{3,2,1,0:T(8,128)(2,1)}), bf16[32,18,16,128]{3,2,1,0:T(8,128)(2,1)}, u32[]{:S(2)}, u32[]{:S(2)}) async-start(bf16[32,18,16,128]{3,2,1,0:T(8,128)(2,1)} %solve_0.6), calls=%async_computation.7 | async-start | bytes 4718592 | tf_op jit(solution)/shard_map/cond/branch_1_fun/all_to_all | solution.py:598
  132.0 32.7 %collective-permute-start.17 = (bf16[1,512,512]{2,1,0:T(8,128)(2,1)S(1)}, bf16[1,512,512]{2,1,0:T(8,128)(2,1)S(1)}, u32[]{:S(2)}, u32[]{:S(2)}) collective-permute-start(bf16[1,512,512]{2,1,0:T(8,128)(2,1)S(1)} %slice.34), channel_id=1, source_target_pairs={{0,2},{1,3},{2,0},{3,1},{4,6},{5,7},{6,4},{7,5},{8,10},{9,11},{10,... | collective-permute-start | bytes 1572872 | tf_op jit(solution)/shard_map/cond/branch_1_fun/ppermute | solution.py:190
  164.6 3.8 %collective-permute-start.21 = (bf16[1,512,512]{2,1,0:T(8,128)(2,1)S(1)}, bf16[1,512,512]{2,1,0:T(8,128)(2,1)S(1)}, u32[]{:S(2)}, u32[]{:S(2)}) collective-permute-start(bf16[1,512,512]{2,1,0:T(8,128)(2,1)S(1)} %collective-permute-done.17.rest_3_), channel_id=1, source_target_pairs={{0,1},{1,0},{2,3},{3,2},{4,5},{5,4},{6,7},{7,6},{8,9},{9,8},{10,11... | collective-permute-start | bytes 1572872 | tf_op jit(solution)/shard_map/cond/branch_1_fun/ppermute | solution.py:190
  183.7 58.7 %all-to-all-start.5 = ((bf16[32,18,16,128]{3,2,1,0:T(8,128)(2,1)}), bf16[32,18,16,128]{3,2,1,0:T(8,128)(2,1)S(1)}, u32[]{:S(2)}, u32[]{:S(2)}) async-start(bf16[32,18,16,128]{3,2,1,0:T(8,128)(2,1)} %solve_1.6), calls=%async_computation.5 | async-start | bytes 4718592 | tf_op jit(solution)/shard_map/cond/branch_1_fun/all_to_all | solution.py:598
  190.5 51.8 %copy-start.9 = (s32[544]{0:T(1024)S(1)}, s32[544]{0:T(1024)}, u32[]{:S(2)}) copy-start(s32[544]{0:T(1024)} %copy-done.8) | copy-start | bytes 6532 | tf_op jit(solution)/shard_map/cond
  194.9 54.2 %collective-permute-start.24 = (bf16[1,544,128]{2,1,0:T(8,128)(2,1)}, bf16[1,544,128]{2,1,0:T(8,128)(2,1)S(1)}, u32[]{:S(2)}, u32[]{:S(2)}) collective-permute-start(bf16[1,544,128]{2,1,0:T(8,128)(2,1)} %get-tuple-element.138), channel_id=1, source_target_pairs={{0,1},{1,2},{2,3},{3,4},{4,5},{5,6},{6,7},{7,8},{8,9},{9,10},{10,1... | collective-permute-start | bytes 417800 | tf_op jit(solution)/shard_map/cond/branch_1_fun/ppermute | solution.py:593
  198.2 50.9 %collective-permute-start.25 = (bf16[1,544,128]{2,1,0:T(8,128)(2,1)}, bf16[1,544,128]{2,1,0:T(8,128)(2,1)S(1)}, u32[]{:S(2)}, u32[]{:S(2)}) collective-permute-start(bf16[1,544,128]{2,1,0:T(8,128)(2,1)} %get-tuple-element.139), channel_id=1, source_target_pairs={{1,0},{2,1},{3,2},{4,3},{5,4},{6,5},{7,6},{8,7},{9,8},{10,9},{11,1... | collective-permute-start | bytes 417800 | tf_op jit(solution)/shard_map/cond/branch_1_fun/ppermute | solution.py:593
  244.1 9.1 %collective-permute-start.26 = (bf16[1,544,128]{2,1,0:T(8,128)(2,1)S(1)}, bf16[1,544,128]{2,1,0:T(8,128)(2,1)S(1)}, u32[]{:S(2)}, u32[]{:S(2)}) collective-permute-start(bf16[1,544,128]{2,1,0:T(8,128)(2,1)S(1)} %get-tuple-element.143), channel_id=1, source_target_pairs={{0,1},{1,2},{2,3},{3,4},{4,5},{5,6},{6,7},{7,8},{8,9},{9,10},{10,1... | collective-permute-start | bytes 417800 | tf_op jit(solution)/shard_map/cond/branch_1_fun/ppermute | solution.py:593
  247.2 8.2 %collective-permute-start.27 = (bf16[1,544,128]{2,1,0:T(8,128)(2,1)S(1)}, bf16[1,544,128]{2,1,0:T(8,128)(2,1)S(1)}, u32[]{:S(2)}, u32[]{:S(2)}) collective-permute-start(bf16[1,544,128]{2,1,0:T(8,128)(2,1)S(1)} %get-tuple-element.144), channel_id=1, source_target_pairs={{1,0},{2,1},{3,2},{4,3},{5,4},{6,5},{7,6},{8,7},{9,8},{10,9},{11,1... | collective-permute-start | bytes 417800 | tf_op jit(solution)/shard_map/cond/branch_1_fun/ppermute | solution.py:593
where the time goes:
time: 259 us; the launch traced here: 257 us
  waiting for transfers between devices  152 us (59%)
  Pallas kernels  59.2 us (23%)
  starting transfers between devices  43.1 us (17%)
    ppermute x9, waiting for transfers between devices, swap(): return lax.ppermute(value, axis, [(i, i ^ bit) for i in range(size)])  107 us
    all_to_all x4, waiting for transfers between devices, exchange(): return lax.all_to_all(shaped, AXES, split_axis=0, concat_axis=0, tiled=True)  43.4 us
    all_to_all x4, starting transfers between devices, exchange(): return lax.all_to_all(shaped, AXES, split_axis=0, concat_axis=0, tiled=True)  26.9 us
    pallas_call x2, Pallas kernels, solve(): pl.pallas_call(functools.partial(solve_kernel, z, f, slots, per_step), gr...  26.8 us
    pallas_call x2, Pallas kernels, pack(): pl.pallas_call(functools.partial(pack_kernel, z, f, slots), in_specs=[sme...  14.6 us
    ppermute x4, starting transfers between devices, beside(): return (lax.ppermute(last, AXES, up), lax.ppermute(first, AXES, down))  10.2 us
    pallas_call x2, Pallas kernels, unpack(): pl.pallas_call(functools.partial(unpack_kernel, z, f), in_specs=[smem, sm...  9.08 us
    pallas_call x2, Pallas kernels, rims(): pl.pallas_call(functools.partial(rim_kernel, z), grid_spec=pltpu.Prefetch...  6.06 us
  transfers between devices with their start and end apart: 18, of which 10 were waited for; matrix products, arithmetic and copies ran while one was open for 0% of the time, Pallas kernels for 20%

commit v1 on v0

--- a/solution.py
+++ b/solution.py
@@ -282,7 +282,7 @@
         out_shape=[jax.ShapeDtypeStruct((total, z.local, z.width), jnp.bfloat16), table],
         scratch_shapes=[
             pltpu.VMEM((z.local, z.blocks, z.width), jnp.bfloat16),
-            pltpu.VMEM((z.local * (z.blocks + 1), z.width), jnp.float32),
+            pltpu.VMEM(((z.local + 1) * (z.blocks + 1), z.width), jnp.float32),
             pltpu.SemaphoreType.DMA((PARTS,)),
         ]
         + [pltpu.SMEM((z.devices,), jnp.int32)] * (0 if f else 2),
@@ -499,7 +499,7 @@
         scratch_shapes=[
             pltpu.VMEM((z.local, z.blocks, z.width), jnp.bfloat16),
             pltpu.VMEM((z.local - 2, z.blocks, z.width), jnp.bfloat16),
-            pltpu.VMEM((z.local * (z.blocks + 1), z.width), jnp.float32),
+            pltpu.VMEM(((z.local + 1) * (z.blocks + 1), z.width), jnp.float32),
             pltpu.SemaphoreType.DMA((2 * PARTS,)),
         ]
         + edge_scratch * min(f, 1),

time: 259 us -> 254 us (0.981); the launches traced: 257 us -> 257 us
  no operation moved by 1% of the time
where the time goes in v1:
time: 254 us; the launch traced here: 257 us
  waiting for transfers between devices  152 us (60%)
  Pallas kernels  59.2 us (23%)
  starting transfers between devices  43.1 us (17%)
    ppermute x9, waiting for transfers between devices, swap(): return lax.ppermute(value, axis, [(i, i ^ bit) for i in range(size)])  106 us
    all_to_all x4, waiting for transfers between devices, exchange(): return lax.all_to_all(shaped, AXES, split_axis=0, concat_axis=0, tiled=True)  43.4 us
    all_to_all x4, starting transfers between devices, exchange(): return lax.all_to_all(shaped, AXES, split_axis=0, concat_axis=0, tiled=True)  26.9 us
    pallas_call x2, Pallas kernels, solve(): pl.pallas_call(functools.partial(solve_kernel, z, f, slots, per_step), gr...  26.8 us
    pallas_call x2, Pallas kernels, pack(): pl.pallas_call(functools.partial(pack_kernel, z, f, slots), in_specs=[sme...  14.6 us
    ppermute x4, starting transfers between devices, beside(): return (lax.ppermute(last, AXES, up), lax.ppermute(first, AXES, down))  10.2 us
    pallas_call x2, Pallas kernels, unpack(): pl.pallas_call(functools.partial(unpack_kernel, z, f), in_specs=[smem, sm...  9.08 us
    pallas_call x2, Pallas kernels, rims(): pl.pallas_call(functools.partial(rim_kernel, z), grid_spec=pltpu.Prefetch...  6.06 us
  transfers between devices with their start and end apart: 18, of which 10 were waited for; matrix products, arithmetic and copies ran while one was open for 0% of the time, Pallas kernels for 20%

profile of v1, /device:TPU:15, one launch (start us, length us, event | category | flops | bytes accessed | tf_op | source)
XLA Modules:
  0.0 256.8 jit_solution(619566249286157778)
XLA Ops:
  0.6 1.9 plan.1
  3.2 253.4 %conditional.1 = (bf16[2,16,544,128]{3,2,1,0:T(8,128)(2,1)}, bf16[2,16,544,128]{3,2,1,0:T(8,128)(2,1)}) conditional(s32[]{:T(128)} %bitcast.30, (s32[64]{0:T(128)}, s32[64]{0:T(128)S(1)}, s32[32]{0:T(128)S(1)}, s32[32]{0:T(128)S(1)}, bf16[2,16,544,128]{3,2,1,0:T(8,128)(2,1)}, ...), branch_computations={%region_0.0_spmd, %region_1.0_spmd, %region_2.0_spmd, %region_3.0_... | conditional | flops 24199999488 | bytes 156327888 | solution.py:612
  3.2 4.8 %pack_0.6 = (bf16[576,16,128]{2,1,0:T(8,128)(2,1)}, s32[544]{0:T(1024)S(1)}) custom-call(s32[64]{0:T(128)} %get-tuple-element.108.refs_0_.start_ref, s32[64]{0:T(128)S(1)} %get-tuple-element.109.refs_1_.mate_ref, s32[32]{0:T(128)S(1)} %get-tuple-element.110.refs_2_, s32[32]{0:T(128)S(1)} %get-tuple-element.111.refs_3_, ...), custom_call_target="tpu_custom_call" | custom-call | flops 1000000000 | bytes 10000000 | tf_op jit(solution)/shard_map/cond/branch_1_fun/pack_0/pallas_call | solution.py:278
  8.0 0.0 copy-start.11
  8.0 6.3 %all-to-all-start.6 = ((bf16[32,18,16,128]{3,2,1,0:T(8,128)(2,1)}), bf16[32,18,16,128]{3,2,1,0:T(8,128)(2,1)}, u32[]{:S(2)}, u32[]{:S(2)}) async-start(bf16[32,18,16,128]{3,2,1,0:T(8,128)(2,1)} %bitcast.10), calls=%async_computation.6 | async-start | bytes 4718592 | tf_op jit(solution)/shard_map/cond/branch_1_fun/all_to_all | solution.py:598
  14.4 0.1 slice_bitcast_fusion.1.rest_0_
  14.5 0.7 collective-permute-start.16
  15.2 0.3 collective-permute-start.15
  15.5 0.3 collective-permute-start.14
  15.8 9.8 %pack_1.6 = (bf16[576,16,128]{2,1,0:T(8,128)(2,1)}, s32[768]{0:T(1024)S(1)}) custom-call(s32[544]{0:T(1024)S(1)} %get-tuple-element.113.refs_0_.place_ref, s32[64]{0:T(128)S(1)} %get-tuple-element.109.refs_1_.mate_ref, bf16[2,16,544,128]{3,2,1,0:T(8,128)(2,1)} %get-tuple-element.287.refs_4_.refs_2_), custom_call_target="tpu_custom_call" | custom-call | flops 1000000000 | bytes 10000000 | tf_op jit(solution)/shard_map/cond/branch_1_fun/pack_1/pallas_call | solution.py:278
  25.6 0.0 collective-permute-done.16.rest_8_
  25.6 38.1 %collective-permute-done.15.rest_2_ = bf16[2,512,512]{2,1,0:T(8,128)(2,1)S(1)} collective-permute-done((bf16[2,512,512]{2,1,0:T(8,128)(2,1)S(1)}, bf16[2,512,512]{2,1,0:T(8,128)(2,1)S(1)}, u32[]{:S(2)}, u32[]{:S(2)}) %collective-permute-start.15) | collective-permute-done | bytes 1048608 | tf_op jit(solution)/shard_map/cond/branch_1_fun/ppermute | solution.py:190
  63.7 0.0 collective-permute-done.14.rest_1_
  63.8 2.6 all-to-all-done.6.columns_ref
  66.3 6.9 %all-to-all-start.4 = ((bf16[32,18,16,128]{3,2,1,0:T(8,128)(2,1)}), bf16[32,18,16,128]{3,2,1,0:T(8,128)(2,1)}, u32[]{:S(2)}, u32[]{:S(2)}) async-start(bf16[32,18,16,128]{3,2,1,0:T(8,128)(2,1)} %bitcast.8), calls=%async_computation.4 | async-start | bytes 4718592 | tf_op jit(solution)/shard_map/cond/branch_1_fun/all_to_all | solution.py:598
  73.3 0.3 collective-permute-start.22
  73.6 0.6 collective-permute-start.19
  74.3 0.0 collective-permute-start.18
  74.3 0.5 collective-permute-start.20
  74.8 32.6 %collective-permute-done.22.rest_3_ = bf16[1,512,512]{2,1,0:T(8,128)(2,1)} collective-permute-done((bf16[1,512,512]{2,1,0:T(8,128)(2,1)S(1)}, bf16[1,512,512]{2,1,0:T(8,128)(2,1)}, u32[]{:S(2)}, u32[]{:S(2)}) %collective-permute-start.22) | collective-permute-done | bytes 524320 | tf_op jit(solution)/shard_map/cond/branch_1_fun/ppermute | solution.py:190
  107.4 0.4 collective-permute-start.23
  107.8 1.9 collective-permute-done.23.rest_7_
  109.7 0.0 collective-permute-done.18.rest_4_
  109.7 0.0 collective-permute-done.19.rest_5_
  109.7 0.0 collective-permute-done.20.rest_6_
  109.7 13.5 %solve_0.6 = bf16[32,18,16,128]{3,2,1,0:T(8,128)(2,1)} custom-call(s32[768]{0:T(1024)S(1)} %get-tuple-element.114.holder_ref, s32[64]{0:T(128)S(1)} %copy-done.16, s32[64]{0:T(128)S(1)} %get-tuple-element.109.refs_1_.mate_ref, s32[1]{0:T(128)} %bitcast.6.me_ref, bf16[32,18,16,128]{3,2,1,0:T(8,128)(2,1)} %all-to-all-done.6.columns_ref, ...), custom_call_target="tpu_custom_call" | custom-call | flops 10000000000 | bytes 10000000 | tf_op jit(solution)/shard_map/cond/branch_1_fun/solve_0/pallas_call | solution.py:372
  123.3 1.7 all-to-all-done.4.columns_ref
  125.0 6.9 %all-to-all-start.7 = ((bf16[32,18,16,128]{3,2,1,0:T(8,128)(2,1)}), bf16[32,18,16,128]{3,2,1,0:T(8,128)(2,1)}, u32[]{:S(2)}, u32[]{:S(2)}) async-start(bf16[32,18,16,128]{3,2,1,0:T(8,128)(2,1)} %solve_0.6), calls=%async_computation.7 | async-start | bytes 4718592 | tf_op jit(solution)/shard_map/cond/branch_1_fun/all_to_all | solution.py:598
  131.9 0.3 collective-permute-start.17
  132.3 32.3 %collective-permute-done.17.rest_3_ = bf16[1,512,512]{2,1,0:T(8,128)(2,1)S(1)} collective-permute-done((bf16[1,512,512]{2,1,0:T(8,128)(2,1)S(1)}, bf16[1,512,512]{2,1,0:T(8,128)(2,1)S(1)}, u32[]{:S(2)}, u32[]{:S(2)}) %collective-permute-start.17) | collective-permute-done | bytes 524320 | tf_op jit(solution)/shard_map/cond/branch_1_fun/ppermute | solution.py:190
  164.6 2.3 collective-permute-start.21
  166.8 1.5 collective-permute-done.21.rest_7_
  168.4 13.3 %solve_1.6 = bf16[32,18,16,128]{3,2,1,0:T(8,128)(2,1)} custom-call(s32[768]{0:T(1024)S(1)} %get-tuple-element.114.holder_ref, s32[64]{0:T(128)S(1)} %copy-done.16, s32[64]{0:T(128)S(1)} %get-tuple-element.109.refs_1_.mate_ref, s32[1]{0:T(128)} %bitcast.6.me_ref, bf16[32,18,16,128]{3,2,1,0:T(8,128)(2,1)} %all-to-all-done.4.columns_ref, ...), custom_call_target="tpu_custom_call" | custom-call | flops 10000000000 | bytes 10000000 | tf_op jit(solution)/shard_map/cond/branch_1_fun/solve_1/pallas_call | solution.py:372
  181.6 2.0 all-to-all-done.7
  183.6 6.8 %all-to-all-start.5 = ((bf16[32,18,16,128]{3,2,1,0:T(8,128)(2,1)}), bf16[32,18,16,128]{3,2,1,0:T(8,128)(2,1)S(1)}, u32[]{:S(2)}, u32[]{:S(2)}) async-start(bf16[32,18,16,128]{3,2,1,0:T(8,128)(2,1)} %solve_1.6), calls=%async_computation.5 | async-start | bytes 4718592 | tf_op jit(solution)/shard_map/cond/branch_1_fun/all_to_all | solution.py:598
  190.5 4.3 %rims_0.6 = (bf16[1,544,128]{2,1,0:T(8,128)(2,1)}, bf16[1,544,128]{2,1,0:T(8,128)(2,1)}) custom-call(s32[544]{0:T(1024)} %copy-done.8, s32[64]{0:T(128)S(1)} %get-tuple-element.109.refs_1_.mate_ref, bf16[576,16,128]{2,1,0:T(8,128)(2,1)} %bitcast.11.returned_ref), custom_call_target="tpu_custom_call" | custom-call | flops 100000000 | bytes 3000000 | tf_op jit(solution)/shard_map/cond/branch_1_fun/rims_0/pallas_call | solution.py:546
  194.8 3.3 %collective-permute-start.24 = (bf16[1,544,128]{2,1,0:T(8,128)(2,1)}, bf16[1,544,128]{2,1,0:T(8,128)(2,1)S(1)}, u32[]{:S(2)}, u32[]{:S(2)}) collective-permute-start(bf16[1,544,128]{2,1,0:T(8,128)(2,1)} %get-tuple-element.138), channel_id=1, source_target_pairs={{0,1},{1,2},{2,3},{3,4},{4,5},{5,6},{6,7},{7,8},{8,9},{9,10},{10,1... | collective-permute-start | bytes 417800 | tf_op jit(solution)/shard_map/cond/branch_1_fun/ppermute | solution.py:593
  198.1 1.9 collective-permute-start.25
  200.1 5.0 %unpack_0.6 = (bf16[2,16,544,128]{3,2,1,0:T(8,128)(2,1)}, bf16[2,16,544,128]{3,2,1,0:T(8,128)(2,1)}) custom-call(s32[544]{0:T(1024)} %copy-done.8, s32[64]{0:T(128)S(1)} %get-tuple-element.109.refs_1_.mate_ref, bf16[576,16,128]{2,1,0:T(8,128)(2,1)} %bitcast.11.returned_ref), custom_call_target="tpu_custom_call" | custom-call | flops 1000000000 | bytes 10000000 | tf_op jit(solution)/shard_map/cond/branch_1_fun/unpack_0/pallas_call | solution.py:494
  205.1 37.2 %all-to-all-done.5 = bf16[32,18,16,128]{3,2,1,0:T(8,128)(2,1)S(1)} async-done(((bf16[32,18,16,128]{3,2,1,0:T(8,128)(2,1)}), bf16[32,18,16,128]{3,2,1,0:T(8,128)(2,1)S(1)}, u32[]{:S(2)}, u32[]{:S(2)}) %all-to-all-start.5) | async-done | bytes 2359328 | tf_op jit(solution)/shard_map/cond/branch_1_fun/all_to_all | solution.py:598
  242.3 1.7 rims_1.6
  244.0 3.1 %collective-permute-start.26 = (bf16[1,544,128]{2,1,0:T(8,128)(2,1)S(1)}, bf16[1,544,128]{2,1,0:T(8,128)(2,1)S(1)}, u32[]{:S(2)}, u32[]{:S(2)}) collective-permute-start(bf16[1,544,128]{2,1,0:T(8,128)(2,1)S(1)} %get-tuple-element.143), channel_id=1, source_target_pairs={{0,1},{1,2},{2,3},{3,4},{4,5},{5,6},{6,7},{7,8},{8,9},{9,10},{10,1... | collective-permute-start | bytes 417800 | tf_op jit(solution)/shard_map/cond/branch_1_fun/ppermute | solution.py:593
  247.1 1.9 collective-permute-start.27
  249.0 0.0 collective-permute-done.24.rest_2_
  249.1 0.0 collective-permute-done.25.rest_3_
  249.1 4.0 %unpack_1.6 = (bf16[2,16,544,128]{3,2,1,0:T(8,128)(2,1)}, bf16[2,16,544,128]{3,2,1,0:T(8,128)(2,1)}, bf16[544,128]{1,0:T(8,128)(2,1)S(1)}, bf16[544,128]{1,0:T(8,128)(2,1)S(1)}) custom-call(s32[544]{0:T(1024)S(1)} %copy-done.9, s32[64]{0:T(128)S(1)} %get-tuple-element.109.refs_1_.mate_ref, ...), custom_call_target="tpu_custom_call", output_to_operand_aliasing={{0}: (3, {}), {1}: (4, {})} | custom-call | flops 1000000000 | bytes 10000000 | tf_op jit(solution)/shard_map/cond/branch_1_fun/unpack_1/pallas_call | solution.py:494
  253.1 2.2 collective-permute-done.27.after_ref
  255.3 0.8 edges_1.6
  (12 shorter events, 0.1 us)
Async XLA Ops:
  8.0 7.8 %copy-start.8 = (s32[544]{0:T(1024)}, s32[544]{0:T(1024)S(1)}, u32[]{:S(2)}) copy-start(s32[544]{0:T(1024)S(1)} %get-tuple-element.113.refs_0_.place_ref) | copy-start | bytes 6532 | tf_op jit(solution)/shard_map/cond
  8.0 6.4 %copy-start.11 = (bf16[2,2,512,512]{3,2,1,0:T(8,128)(2,1)S(1)}, bf16[2,2,512,512]{3,2,1,0:T(8,128)(2,1)}, u32[]{:S(2)}) copy-start(bf16[2,2,512,512]{3,2,1,0:T(8,128)(2,1)} %get-tuple-element.330.inverses_ref) | copy-start | bytes 6291460 | tf_op jit(solution)/shard_map/cond
  8.0 58.3 %all-to-all-start.6 = ((bf16[32,18,16,128]{3,2,1,0:T(8,128)(2,1)}), bf16[32,18,16,128]{3,2,1,0:T(8,128)(2,1)}, u32[]{:S(2)}, u32[]{:S(2)}) async-start(bf16[32,18,16,128]{3,2,1,0:T(8,128)(2,1)} %bitcast.10), calls=%async_computation.6 | async-start | bytes 4718592 | tf_op jit(solution)/shard_map/cond/branch_1_fun/all_to_all | solution.py:598
  14.5 11.1 %collective-permute-start.16 = (bf16[2,512,512]{2,1,0:T(8,128)(2,1)S(1)}, bf16[2,512,512]{2,1,0:T(8,128)(2,1)S(1)}, u32[]{:S(2)}, u32[]{:S(2)}) collective-permute-start(bf16[2,512,512]{2,1,0:T(8,128)(2,1)S(1)} %slice_bitcast_fusion.1.rest_0_), channel_id=1, source_target_pairs={{0,8},{2,10},{4,12},{6,14},{8,0},{10,2},{12,4},{14,6},{16,24},{18,... | collective-permute-start | bytes 3145736 | tf_op jit(solution)/shard_map/cond/branch_1_fun/ppermute | solution.py:197
  15.2 48.6 %collective-permute-start.15 = (bf16[2,512,512]{2,1,0:T(8,128)(2,1)S(1)}, bf16[2,512,512]{2,1,0:T(8,128)(2,1)S(1)}, u32[]{:S(2)}, u32[]{:S(2)}) collective-permute-start(bf16[2,512,512]{2,1,0:T(8,128)(2,1)S(1)} %slice_bitcast_fusion.1.rest_0_), channel_id=1, source_target_pairs={{0,4},{4,0},{8,12},{12,8},{16,20},{20,16},{24,28},{28,24},{1,5},{5... | collective-permute-start | bytes 3145736 | tf_op jit(solution)/shard_map/cond/branch_1_fun/ppermute | solution.py:190
  15.5 48.2 %collective-permute-start.14 = (bf16[2,512,512]{2,1,0:T(8,128)(2,1)S(1)}, bf16[2,512,512]{2,1,0:T(8,128)(2,1)S(1)}, u32[]{:S(2)}, u32[]{:S(2)}) collective-permute-start(bf16[2,512,512]{2,1,0:T(8,128)(2,1)S(1)} %slice_bitcast_fusion.1.rest_0_), channel_id=1, source_target_pairs={{0,2},{1,3},{2,0},{3,1},{4,6},{5,7},{6,4},{7,5},{8,10},{9,11},{10,... | collective-permute-start | bytes 3145736 | tf_op jit(solution)/shard_map/cond/branch_1_fun/ppermute | solution.py:190
  25.6 38.1 %copy-start.21 = (bf16[2,512,512]{2,1,0:T(8,128)(2,1)}, bf16[2,512,512]{2,1,0:T(8,128)(2,1)S(1)}, u32[]{:S(2)}) copy-start(bf16[2,512,512]{2,1,0:T(8,128)(2,1)S(1)} %collective-permute-done.16.rest_8_) | copy-start | bytes 3145732 | tf_op jit(solution)/shard_map/cond
  66.3 43.4 %copy-start.16 = (s32[64]{0:T(128)S(1)}, s32[64]{0:T(128)}, u32[]{:S(2)}) copy-start(s32[64]{0:T(128)} %get-tuple-element.108.refs_0_.start_ref) | copy-start | bytes 772 | tf_op jit(solution)/shard_map/cond
  66.3 58.7 %all-to-all-start.4 = ((bf16[32,18,16,128]{3,2,1,0:T(8,128)(2,1)}), bf16[32,18,16,128]{3,2,1,0:T(8,128)(2,1)}, u32[]{:S(2)}, u32[]{:S(2)}) async-start(bf16[32,18,16,128]{3,2,1,0:T(8,128)(2,1)} %bitcast.8), calls=%async_computation.4 | async-start | bytes 4718592 | tf_op jit(solution)/shard_map/cond/branch_1_fun/all_to_all | solution.py:598
  73.3 34.1 %collective-permute-start.22 = (bf16[1,512,512]{2,1,0:T(8,128)(2,1)S(1)}, bf16[1,512,512]{2,1,0:T(8,128)(2,1)}, u32[]{:S(2)}, u32[]{:S(2)}) collective-permute-start(bf16[1,512,512]{2,1,0:T(8,128)(2,1)S(1)} %slice.35), channel_id=1, source_target_pairs={{0,4},{4,0},{8,12},{12,8},{16,20},{20,16},{24,28},{28,24},{1,5},{5... | collective-permute-start | bytes 1572872 | tf_op jit(solution)/shard_map/cond/branch_1_fun/ppermute | solution.py:190
  73.6 36.1 %collective-permute-start.19 = (bf16[2,512,512]{2,1,0:T(8,128)(2,1)S(1)}, bf16[2,512,512]{2,1,0:T(8,128)(2,1)}, u32[]{:S(2)}, u32[]{:S(2)}) collective-permute-start(bf16[2,512,512]{2,1,0:T(8,128)(2,1)S(1)} %collective-permute-done.14.rest_1_), channel_id=1, source_target_pairs={{0,1},{1,0},{2,3},{3,2},{4,5},{5,4},{6,7},{7,6},{8,9},{9,8},{10,11... | collective-permute-start | bytes 3145736 | tf_op jit(solution)/shard_map/cond/branch_1_fun/ppermute | solution.py:190
  74.3 35.5 %collective-permute-start.18 = (bf16[2,512,512]{2,1,0:T(8,128)(2,1)S(1)}, bf16[2,512,512]{2,1,0:T(8,128)(2,1)}, u32[]{:S(2)}, u32[]{:S(2)}) collective-permute-start(bf16[2,512,512]{2,1,0:T(8,128)(2,1)S(1)} %slice_bitcast_fusion.1.rest_0_), channel_id=1, source_target_pairs={{0,1},{1,0},{2,3},{3,2},{4,5},{5,4},{6,7},{7,6},{8,9},{9,8},{10,11... | collective-permute-start | bytes 3145736 | tf_op jit(solution)/shard_map/cond/branch_1_fun/ppermute | solution.py:190
  74.3 35.5 %collective-permute-start.20 = (bf16[2,512,512]{2,1,0:T(8,128)(2,1)S(1)}, bf16[2,512,512]{2,1,0:T(8,128)(2,1)}, u32[]{:S(2)}, u32[]{:S(2)}) collective-permute-start(bf16[2,512,512]{2,1,0:T(8,128)(2,1)S(1)} %collective-permute-done.15.rest_2_), channel_id=1, source_target_pairs={{0,1},{1,0},{2,3},{3,2},{4,5},{5,4},{6,7},{7,6},{8,9},{9,8},{10,11... | collective-permute-start | bytes 3145736 | tf_op jit(solution)/shard_map/cond/branch_1_fun/ppermute | solution.py:190
  107.4 2.3 collective-permute-start.23
  125.0 58.7 %all-to-all-start.7 = ((bf16[32,18,16,128]{3,2,1,0:T(8,128)(2,1)}), bf16[32,18,16,128]{3,2,1,0:T(8,128)(2,1)}, u32[]{:S(2)}, u32[]{:S(2)}) async-start(bf16[32,18,16,128]{3,2,1,0:T(8,128)(2,1)} %solve_0.6), calls=%async_computation.7 | async-start | bytes 4718592 | tf_op jit(solution)/shard_map/cond/branch_1_fun/all_to_all | solution.py:598
  131.9 32.7 %collective-permute-start.17 = (bf16[1,512,512]{2,1,0:T(8,128)(2,1)S(1)}, bf16[1,512,512]{2,1,0:T(8,128)(2,1)S(1)}, u32[]{:S(2)}, u32[]{:S(2)}) collective-permute-start(bf16[1,512,512]{2,1,0:T(8,128)(2,1)S(1)} %slice.34), channel_id=1, source_target_pairs={{0,2},{1,3},{2,0},{3,1},{4,6},{5,7},{6,4},{7,5},{8,10},{9,11},{10,... | collective-permute-start | bytes 1572872 | tf_op jit(solution)/shard_map/cond/branch_1_fun/ppermute | solution.py:190
  164.6 3.8 %collective-permute-start.21 = (bf16[1,512,512]{2,1,0:T(8,128)(2,1)S(1)}, bf16[1,512,512]{2,1,0:T(8,128)(2,1)S(1)}, u32[]{:S(2)}, u32[]{:S(2)}) collective-permute-start(bf16[1,512,512]{2,1,0:T(8,128)(2,1)S(1)} %collective-permute-done.17.rest_3_), channel_id=1, source_target_pairs={{0,1},{1,0},{2,3},{3,2},{4,5},{5,4},{6,7},{7,6},{8,9},{9,8},{10,11... | collective-permute-start | bytes 1572872 | tf_op jit(solution)/shard_map/cond/branch_1_fun/ppermute | solution.py:190
  183.6 58.7 %all-to-all-start.5 = ((bf16[32,18,16,128]{3,2,1,0:T(8,128)(2,1)}), bf16[32,18,16,128]{3,2,1,0:T(8,128)(2,1)S(1)}, u32[]{:S(2)}, u32[]{:S(2)}) async-start(bf16[32,18,16,128]{3,2,1,0:T(8,128)(2,1)} %solve_1.6), calls=%async_computation.5 | async-start | bytes 4718592 | tf_op jit(solution)/shard_map/cond/branch_1_fun/all_to_all | solution.py:598
  190.5 51.8 %copy-start.9 = (s32[544]{0:T(1024)S(1)}, s32[544]{0:T(1024)}, u32[]{:S(2)}) copy-start(s32[544]{0:T(1024)} %copy-done.8) | copy-start | bytes 6532 | tf_op jit(solution)/shard_map/cond
  194.8 54.2 %collective-permute-start.24 = (bf16[1,544,128]{2,1,0:T(8,128)(2,1)}, bf16[1,544,128]{2,1,0:T(8,128)(2,1)S(1)}, u32[]{:S(2)}, u32[]{:S(2)}) collective-permute-start(bf16[1,544,128]{2,1,0:T(8,128)(2,1)} %get-tuple-element.138), channel_id=1, source_target_pairs={{0,1},{1,2},{2,3},{3,4},{4,5},{5,6},{6,7},{7,8},{8,9},{9,10},{10,1... | collective-permute-start | bytes 417800 | tf_op jit(solution)/shard_map/cond/branch_1_fun/ppermute | solution.py:593
  198.1 50.9 %collective-permute-start.25 = (bf16[1,544,128]{2,1,0:T(8,128)(2,1)}, bf16[1,544,128]{2,1,0:T(8,128)(2,1)S(1)}, u32[]{:S(2)}, u32[]{:S(2)}) collective-permute-start(bf16[1,544,128]{2,1,0:T(8,128)(2,1)} %get-tuple-element.139), channel_id=1, source_target_pairs={{1,0},{2,1},{3,2},{4,3},{5,4},{6,5},{7,6},{8,7},{9,8},{10,9},{11,1... | collective-permute-start | bytes 417800 | tf_op jit(solution)/shard_map/cond/branch_1_fun/ppermute | solution.py:593
  244.0 9.1 %collective-permute-start.26 = (bf16[1,544,128]{2,1,0:T(8,128)(2,1)S(1)}, bf16[1,544,128]{2,1,0:T(8,128)(2,1)S(1)}, u32[]{:S(2)}, u32[]{:S(2)}) collective-permute-start(bf16[1,544,128]{2,1,0:T(8,128)(2,1)S(1)} %get-tuple-element.143), channel_id=1, source_target_pairs={{0,1},{1,2},{2,3},{3,4},{4,5},{5,6},{6,7},{7,8},{8,9},{9,10},{10,1... | collective-permute-start | bytes 417800 | tf_op jit(solution)/shard_map/cond/branch_1_fun/ppermute | solution.py:593
  247.1 8.2 %collective-permute-start.27 = (bf16[1,544,128]{2,1,0:T(8,128)(2,1)S(1)}, bf16[1,544,128]{2,1,0:T(8,128)(2,1)S(1)}, u32[]{:S(2)}, u32[]{:S(2)}) collective-permute-start(bf16[1,544,128]{2,1,0:T(8,128)(2,1)S(1)} %get-tuple-element.144), channel_id=1, source_target_pairs={{1,0},{2,1},{3,2},{4,3},{5,4},{6,5},{7,6},{8,7},{9,8},{10,9},{11,1... | collective-permute-start | bytes 417800 | tf_op jit(solution)/shard_map/cond/branch_1_fun/ppermute | solution.py:593

commit v2 on v1

--- a/solution.py
+++ b/solution.py
@@ -14,10 +14,10 @@
 PLANE = 8
 GIFT = 8
 GROUP = 16
-BATCH = 34
+BATCH = 68
 VMEM = 48 << 20
 MORE_VMEM = 60 << 20
-RIDES = 16
+RIDES = 32
 PARTS = 4
 
 inner_radius = 0.35
@@ -365,7 +365,7 @@
 
 
 def solve(z, holder, degree_start, mate, me, columns, inverses, pieces, f, slots):
-    steps = pl.cdiv(slots, 5)
+    steps = pl.cdiv(slots, 9)
     per_step = pl.cdiv(slots, steps)
     block = (z.devices, per_step, z.local, z.width)
     spec = pl.BlockSpec(block, lambda i, *s: (0, i, 0, 0))
@@ -453,7 +453,7 @@
     copies = []
     for i in range(PARTS):
         begin, end = i * groups // PARTS, (i + 1) * groups // PARTS
-        lax.fori_loop(begin, end, group, 0)
+        lax.fori_loop(begin, end, group, 0, unroll=2)
         rows = pl.ds(begin * GROUP, (end - begin) * GROUP)
         copies += [
             pltpu.make_async_copy(
@@ -602,7 +602,7 @@
     rad, lm = lax.axis_size("rad"), lax.axis_size("lm")
     z = Sizes(rad * lm, grid_field, inverses, slot_blocks)
     choices = slot_choices(z)
-    kernels = z.local % 16 == 0 and z.fields == 2 and z.blocks % GROUP == 0 and rad % 4 == 0 and lm == PLANE // 2
+    kernels = z.local % 16 == 0 and z.fields == 2 and z.blocks % GROUP == 0 and z.blocks % BATCH == 0 and rad % 4 == 0 and lm == PLANE // 2
     low, high = z.counts[z.degrees // 2 - 1 : z.degrees // 2 + 1]
     if not kernels or low + GIFT > choices[0] or high <= GIFT or z.capacity - choices[0] > GIFT:
         return plain_body(z, grid_field, inverses, degree_start)

time: 254 us -> 259 us (1.020); the launches traced: 257 us -> 256 us
  transfers between devices with their start and end apart: 18 -> 18, of which waited for: 10 -> 10; matrix products, arithmetic and copies ran while one was open for 0% -> 0% of each run, Pallas kernels for 20% -> 19%
where the time goes in v2:
time: 259 us; the launch traced here: 256 us
  waiting for transfers between devices  154 us (59%)
  Pallas kernels  57 us (22%)
  starting transfers between devices  43.3 us (17%)
    ppermute x9, waiting for transfers between devices, swap(): return lax.ppermute(value, axis, [(i, i ^ bit) for i in range(size)])  106 us
    all_to_all x4, waiting for transfers between devices, exchange(): return lax.all_to_all(shaped, AXES, split_axis=0, concat_axis=0, tiled=True)  44.7 us
    all_to_all x4, starting transfers between devices, exchange(): return lax.all_to_all(shaped, AXES, split_axis=0, concat_axis=0, tiled=True)  26.9 us
    pallas_call x2, Pallas kernels, solve(): pl.pallas_call(functools.partial(solve_kernel, z, f, slots, per_step), gr...  25.9 us
    pallas_call x2, Pallas kernels, pack(): pl.pallas_call(functools.partial(pack_kernel, z, f, slots), in_specs=[sme...  14.2 us
    ppermute x4, starting transfers between devices, beside(): return (lax.ppermute(last, AXES, up), lax.ppermute(first, AXES, down))  10.2 us
    pallas_call x2, Pallas kernels, unpack(): pl.pallas_call(functools.partial(unpack_kernel, z, f), in_specs=[smem, sm...  8.61 us
    pallas_call x2, Pallas kernels, rims(): pl.pallas_call(functools.partial(rim_kernel, z), grid_spec=pltpu.Prefetch...  5.67 us
  transfers between devices with their start and end apart: 18, of which 10 were waited for; matrix products, arithmetic and copies ran while one was open for 0% of the time, Pallas kernels for 19%

profile of v2, /device:TPU:15, one launch (start us, length us, event | category | flops | bytes accessed | tf_op | source)
XLA Modules:
  0.0 256.4 jit_solution(14008044782064618129)
XLA Ops:
  0.6 1.9 plan.1
  3.2 253.0 %conditional.1 = (bf16[2,16,544,128]{3,2,1,0:T(8,128)(2,1)}, bf16[2,16,544,128]{3,2,1,0:T(8,128)(2,1)}) conditional(s32[]{:T(128)} %bitcast.30, (s32[64]{0:T(128)}, s32[64]{0:T(128)S(1)}, s32[32]{0:T(128)S(1)}, s32[32]{0:T(128)S(1)}, bf16[2,16,544,128]{3,2,1,0:T(8,128)(2,1)}, ...), branch_computations={%region_0.0_spmd, %region_1.0_spmd, %region_2.0_spmd, %region_3.0_... | conditional | flops 24199999488 | bytes 156327888 | solution.py:612
  3.2 4.6 %pack_0.6 = (bf16[576,16,128]{2,1,0:T(8,128)(2,1)}, s32[544]{0:T(1024)S(1)}) custom-call(s32[64]{0:T(128)} %get-tuple-element.108.refs_0_.start_ref, s32[64]{0:T(128)S(1)} %get-tuple-element.109.refs_1_.mate_ref, s32[32]{0:T(128)S(1)} %get-tuple-element.110.refs_2_, s32[32]{0:T(128)S(1)} %get-tuple-element.111.refs_3_, ...), custom_call_target="tpu_custom_call" | custom-call | flops 1000000000 | bytes 10000000 | tf_op jit(solution)/shard_map/cond/branch_1_fun/pack_0/pallas_call | solution.py:278
  7.8 0.0 copy-start.11
  7.8 6.3 %all-to-all-start.6 = ((bf16[32,18,16,128]{3,2,1,0:T(8,128)(2,1)}), bf16[32,18,16,128]{3,2,1,0:T(8,128)(2,1)}, u32[]{:S(2)}, u32[]{:S(2)}) async-start(bf16[32,18,16,128]{3,2,1,0:T(8,128)(2,1)} %bitcast.10), calls=%async_computation.6 | async-start | bytes 4718592 | tf_op jit(solution)/shard_map/cond/branch_1_fun/all_to_all | solution.py:598
  14.2 0.1 slice_bitcast_fusion.1.rest_0_
  14.3 0.9 collective-permute-start.16
  15.2 0.3 collective-permute-start.15
  15.5 0.3 collective-permute-start.14
  15.8 9.6 %pack_1.6 = (bf16[576,16,128]{2,1,0:T(8,128)(2,1)}, s32[768]{0:T(1024)S(1)}) custom-call(s32[544]{0:T(1024)S(1)} %get-tuple-element.113.refs_0_.place_ref, s32[64]{0:T(128)S(1)} %get-tuple-element.109.refs_1_.mate_ref, bf16[2,16,544,128]{3,2,1,0:T(8,128)(2,1)} %get-tuple-element.287.refs_4_.refs_2_), custom_call_target="tpu_custom_call" | custom-call | flops 1000000000 | bytes 10000000 | tf_op jit(solution)/shard_map/cond/branch_1_fun/pack_1/pallas_call | solution.py:278
  25.4 0.0 collective-permute-done.16.rest_8_
  25.4 38.1 %collective-permute-done.15.rest_2_ = bf16[2,512,512]{2,1,0:T(8,128)(2,1)S(1)} collective-permute-done((bf16[2,512,512]{2,1,0:T(8,128)(2,1)S(1)}, bf16[2,512,512]{2,1,0:T(8,128)(2,1)S(1)}, u32[]{:S(2)}, u32[]{:S(2)}) %collective-permute-start.15) | collective-permute-done | bytes 1048608 | tf_op jit(solution)/shard_map/cond/branch_1_fun/ppermute | solution.py:190
  63.5 0.0 collective-permute-done.14.rest_1_
  63.6 2.6 all-to-all-done.6.columns_ref
  66.1 6.9 %all-to-all-start.4 = ((bf16[32,18,16,128]{3,2,1,0:T(8,128)(2,1)}), bf16[32,18,16,128]{3,2,1,0:T(8,128)(2,1)}, u32[]{:S(2)}, u32[]{:S(2)}) async-start(bf16[32,18,16,128]{3,2,1,0:T(8,128)(2,1)} %bitcast.8), calls=%async_computation.4 | async-start | bytes 4718592 | tf_op jit(solution)/shard_map/cond/branch_1_fun/all_to_all | solution.py:598
  73.1 0.3 collective-permute-start.22
  73.4 0.6 collective-permute-start.19
  74.0 0.0 collective-permute-start.18
  74.0 0.5 collective-permute-start.20
  74.6 32.6 %collective-permute-done.22.rest_3_ = bf16[1,512,512]{2,1,0:T(8,128)(2,1)} collective-permute-done((bf16[1,512,512]{2,1,0:T(8,128)(2,1)S(1)}, bf16[1,512,512]{2,1,0:T(8,128)(2,1)}, u32[]{:S(2)}, u32[]{:S(2)}) %collective-permute-start.22) | collective-permute-done | bytes 524320 | tf_op jit(solution)/shard_map/cond/branch_1_fun/ppermute | solution.py:190
  107.2 0.4 collective-permute-start.23
  107.6 1.9 collective-permute-done.23.rest_7_
  109.5 0.0 collective-permute-done.18.rest_4_
  109.5 0.0 collective-permute-done.19.rest_5_
  109.5 0.0 collective-permute-done.20.rest_6_
  109.5 13.1 %solve_0.6 = bf16[32,18,16,128]{3,2,1,0:T(8,128)(2,1)} custom-call(s32[768]{0:T(1024)S(1)} %get-tuple-element.114.holder_ref, s32[64]{0:T(128)S(1)} %copy-done.16, s32[64]{0:T(128)S(1)} %get-tuple-element.109.refs_1_.mate_ref, s32[1]{0:T(128)} %bitcast.6.me_ref, bf16[32,18,16,128]{3,2,1,0:T(8,128)(2,1)} %all-to-all-done.6.columns_ref, ...), custom_call_target="tpu_custom_call" | custom-call | flops 10000000000 | bytes 10000000 | tf_op jit(solution)/shard_map/cond/branch_1_fun/solve_0/pallas_call | solution.py:372
  122.6 2.1 all-to-all-done.4.columns_ref
  124.8 6.9 %all-to-all-start.7 = ((bf16[32,18,16,128]{3,2,1,0:T(8,128)(2,1)}), bf16[32,18,16,128]{3,2,1,0:T(8,128)(2,1)}, u32[]{:S(2)}, u32[]{:S(2)}) async-start(bf16[32,18,16,128]{3,2,1,0:T(8,128)(2,1)} %solve_0.6), calls=%async_computation.7 | async-start | bytes 4718592 | tf_op jit(solution)/shard_map/cond/branch_1_fun/all_to_all | solution.py:598
  131.7 0.3 collective-permute-start.17
  132.1 32.3 %collective-permute-done.17.rest_3_ = bf16[1,512,512]{2,1,0:T(8,128)(2,1)S(1)} collective-permute-done((bf16[1,512,512]{2,1,0:T(8,128)(2,1)S(1)}, bf16[1,512,512]{2,1,0:T(8,128)(2,1)S(1)}, u32[]{:S(2)}, u32[]{:S(2)}) %collective-permute-start.17) | collective-permute-done | bytes 524320 | tf_op jit(solution)/shard_map/cond/branch_1_fun/ppermute | solution.py:190
  164.4 2.3 collective-permute-start.21
  166.6 1.5 collective-permute-done.21.rest_7_
  168.2 12.8 %solve_1.6 = bf16[32,18,16,128]{3,2,1,0:T(8,128)(2,1)} custom-call(s32[768]{0:T(1024)S(1)} %get-tuple-element.114.holder_ref, s32[64]{0:T(128)S(1)} %copy-done.16, s32[64]{0:T(128)S(1)} %get-tuple-element.109.refs_1_.mate_ref, s32[1]{0:T(128)} %bitcast.6.me_ref, bf16[32,18,16,128]{3,2,1,0:T(8,128)(2,1)} %all-to-all-done.4.columns_ref, ...), custom_call_target="tpu_custom_call" | custom-call | flops 10000000000 | bytes 10000000 | tf_op jit(solution)/shard_map/cond/branch_1_fun/solve_1/pallas_call | solution.py:372
  181.0 2.4 all-to-all-done.7
  183.4 6.8 %all-to-all-start.5 = ((bf16[32,18,16,128]{3,2,1,0:T(8,128)(2,1)}), bf16[32,18,16,128]{3,2,1,0:T(8,128)(2,1)S(1)}, u32[]{:S(2)}, u32[]{:S(2)}) async-start(bf16[32,18,16,128]{3,2,1,0:T(8,128)(2,1)} %solve_1.6), calls=%async_computation.5 | async-start | bytes 4718592 | tf_op jit(solution)/shard_map/cond/branch_1_fun/all_to_all | solution.py:598
  190.3 4.1 %rims_0.6 = (bf16[1,544,128]{2,1,0:T(8,128)(2,1)}, bf16[1,544,128]{2,1,0:T(8,128)(2,1)}) custom-call(s32[544]{0:T(1024)} %copy-done.8, s32[64]{0:T(128)S(1)} %get-tuple-element.109.refs_1_.mate_ref, bf16[576,16,128]{2,1,0:T(8,128)(2,1)} %bitcast.11.returned_ref), custom_call_target="tpu_custom_call" | custom-call | flops 100000000 | bytes 3000000 | tf_op jit(solution)/shard_map/cond/branch_1_fun/rims_0/pallas_call | solution.py:546
  194.4 3.3 %collective-permute-start.24 = (bf16[1,544,128]{2,1,0:T(8,128)(2,1)}, bf16[1,544,128]{2,1,0:T(8,128)(2,1)S(1)}, u32[]{:S(2)}, u32[]{:S(2)}) collective-permute-start(bf16[1,544,128]{2,1,0:T(8,128)(2,1)} %get-tuple-element.138), channel_id=1, source_target_pairs={{0,1},{1,2},{2,3},{3,4},{4,5},{5,6},{6,7},{7,8},{8,9},{9,10},{10,1... | collective-permute-start | bytes 417800 | tf_op jit(solution)/shard_map/cond/branch_1_fun/ppermute | solution.py:593
  197.7 1.9 collective-permute-start.25
  199.7 4.8 %unpack_0.6 = (bf16[2,16,544,128]{3,2,1,0:T(8,128)(2,1)}, bf16[2,16,544,128]{3,2,1,0:T(8,128)(2,1)}) custom-call(s32[544]{0:T(1024)} %copy-done.8, s32[64]{0:T(128)S(1)} %get-tuple-element.109.refs_1_.mate_ref, bf16[576,16,128]{2,1,0:T(8,128)(2,1)} %bitcast.11.returned_ref), custom_call_target="tpu_custom_call" | custom-call | flops 1000000000 | bytes 10000000 | tf_op jit(solution)/shard_map/cond/branch_1_fun/unpack_0/pallas_call | solution.py:494
  204.5 37.6 %all-to-all-done.5 = bf16[32,18,16,128]{3,2,1,0:T(8,128)(2,1)S(1)} async-done(((bf16[32,18,16,128]{3,2,1,0:T(8,128)(2,1)}), bf16[32,18,16,128]{3,2,1,0:T(8,128)(2,1)S(1)}, u32[]{:S(2)}, u32[]{:S(2)}) %all-to-all-start.5) | async-done | bytes 2359328 | tf_op jit(solution)/shard_map/cond/branch_1_fun/all_to_all | solution.py:598
  242.1 1.5 rims_1.6
  243.6 3.1 %collective-permute-start.26 = (bf16[1,544,128]{2,1,0:T(8,128)(2,1)S(1)}, bf16[1,544,128]{2,1,0:T(8,128)(2,1)S(1)}, u32[]{:S(2)}, u32[]{:S(2)}) collective-permute-start(bf16[1,544,128]{2,1,0:T(8,128)(2,1)S(1)} %get-tuple-element.143), channel_id=1, source_target_pairs={{0,1},{1,2},{2,3},{3,4},{4,5},{5,6},{6,7},{7,8},{8,9},{9,10},{10,1... | collective-permute-start | bytes 417800 | tf_op jit(solution)/shard_map/cond/branch_1_fun/ppermute | solution.py:593
  246.7 1.9 collective-permute-start.27
  248.6 0.0 collective-permute-done.25.rest_3_
  248.7 3.8 %unpack_1.6 = (bf16[2,16,544,128]{3,2,1,0:T(8,128)(2,1)}, bf16[2,16,544,128]{3,2,1,0:T(8,128)(2,1)}, bf16[544,128]{1,0:T(8,128)(2,1)S(1)}, bf16[544,128]{1,0:T(8,128)(2,1)S(1)}) custom-call(s32[544]{0:T(1024)S(1)} %copy-done.9, s32[64]{0:T(128)S(1)} %get-tuple-element.109.refs_1_.mate_ref, ...), custom_call_target="tpu_custom_call", output_to_operand_aliasing={{0}: (3, {}), {1}: (4, {})} | custom-call | flops 1000000000 | bytes 10000000 | tf_op jit(solution)/shard_map/cond/branch_1_fun/unpack_1/pallas_call | solution.py:494
  252.5 0.0 collective-permute-done.26.before_ref
  252.5 2.4 collective-permute-done.27.after_ref
  254.9 0.8 edges_1.6
  (12 shorter events, 0.1 us)
Async XLA Ops:
  7.8 8.0 %copy-start.8 = (s32[544]{0:T(1024)}, s32[544]{0:T(1024)S(1)}, u32[]{:S(2)}) copy-start(s32[544]{0:T(1024)S(1)} %get-tuple-element.113.refs_0_.place_ref) | copy-start | bytes 6532 | tf_op jit(solution)/shard_map/cond
  7.8 6.4 %copy-start.11 = (bf16[2,2,512,512]{3,2,1,0:T(8,128)(2,1)S(1)}, bf16[2,2,512,512]{3,2,1,0:T(8,128)(2,1)}, u32[]{:S(2)}) copy-start(bf16[2,2,512,512]{3,2,1,0:T(8,128)(2,1)} %get-tuple-element.330.inverses_ref) | copy-start | bytes 6291460 | tf_op jit(solution)/shard_map/cond
  7.8 58.3 %all-to-all-start.6 = ((bf16[32,18,16,128]{3,2,1,0:T(8,128)(2,1)}), bf16[32,18,16,128]{3,2,1,0:T(8,128)(2,1)}, u32[]{:S(2)}, u32[]{:S(2)}) async-start(bf16[32,18,16,128]{3,2,1,0:T(8,128)(2,1)} %bitcast.10), calls=%async_computation.6 | async-start | bytes 4718592 | tf_op jit(solution)/shard_map/cond/branch_1_fun/all_to_all | solution.py:598
  14.3 11.2 %collective-permute-start.16 = (bf16[2,512,512]{2,1,0:T(8,128)(2,1)S(1)}, bf16[2,512,512]{2,1,0:T(8,128)(2,1)S(1)}, u32[]{:S(2)}, u32[]{:S(2)}) collective-permute-start(bf16[2,512,512]{2,1,0:T(8,128)(2,1)S(1)} %slice_bitcast_fusion.1.rest_0_), channel_id=1, source_target_pairs={{0,8},{2,10},{4,12},{6,14},{8,0},{10,2},{12,4},{14,6},{16,24},{18,... | collective-permute-start | bytes 3145736 | tf_op jit(solution)/shard_map/cond/branch_1_fun/ppermute | solution.py:197
  15.2 48.4 %collective-permute-start.15 = (bf16[2,512,512]{2,1,0:T(8,128)(2,1)S(1)}, bf16[2,512,512]{2,1,0:T(8,128)(2,1)S(1)}, u32[]{:S(2)}, u32[]{:S(2)}) collective-permute-start(bf16[2,512,512]{2,1,0:T(8,128)(2,1)S(1)} %slice_bitcast_fusion.1.rest_0_), channel_id=1, source_target_pairs={{0,4},{4,0},{8,12},{12,8},{16,20},{20,16},{24,28},{28,24},{1,5},{5... | collective-permute-start | bytes 3145736 | tf_op jit(solution)/shard_map/cond/branch_1_fun/ppermute | solution.py:190
  15.5 48.0 %collective-permute-start.14 = (bf16[2,512,512]{2,1,0:T(8,128)(2,1)S(1)}, bf16[2,512,512]{2,1,0:T(8,128)(2,1)S(1)}, u32[]{:S(2)}, u32[]{:S(2)}) collective-permute-start(bf16[2,512,512]{2,1,0:T(8,128)(2,1)S(1)} %slice_bitcast_fusion.1.rest_0_), channel_id=1, source_target_pairs={{0,2},{1,3},{2,0},{3,1},{4,6},{5,7},{6,4},{7,5},{8,10},{9,11},{10,... | collective-permute-start | bytes 3145736 | tf_op jit(solution)/shard_map/cond/branch_1_fun/ppermute | solution.py:190
  25.4 38.1 %copy-start.21 = (bf16[2,512,512]{2,1,0:T(8,128)(2,1)}, bf16[2,512,512]{2,1,0:T(8,128)(2,1)S(1)}, u32[]{:S(2)}) copy-start(bf16[2,512,512]{2,1,0:T(8,128)(2,1)S(1)} %collective-permute-done.16.rest_8_) | copy-start | bytes 3145732 | tf_op jit(solution)/shard_map/cond
  66.1 43.4 %copy-start.16 = (s32[64]{0:T(128)S(1)}, s32[64]{0:T(128)}, u32[]{:S(2)}) copy-start(s32[64]{0:T(128)} %get-tuple-element.108.refs_0_.start_ref) | copy-start | bytes 772 | tf_op jit(solution)/shard_map/cond
  66.1 58.7 %all-to-all-start.4 = ((bf16[32,18,16,128]{3,2,1,0:T(8,128)(2,1)}), bf16[32,18,16,128]{3,2,1,0:T(8,128)(2,1)}, u32[]{:S(2)}, u32[]{:S(2)}) async-start(bf16[32,18,16,128]{3,2,1,0:T(8,128)(2,1)} %bitcast.8), calls=%async_computation.4 | async-start | bytes 4718592 | tf_op jit(solution)/shard_map/cond/branch_1_fun/all_to_all | solution.py:598
  73.1 34.1 %collective-permute-start.22 = (bf16[1,512,512]{2,1,0:T(8,128)(2,1)S(1)}, bf16[1,512,512]{2,1,0:T(8,128)(2,1)}, u32[]{:S(2)}, u32[]{:S(2)}) collective-permute-start(bf16[1,512,512]{2,1,0:T(8,128)(2,1)S(1)} %slice.35), channel_id=1, source_target_pairs={{0,4},{4,0},{8,12},{12,8},{16,20},{20,16},{24,28},{28,24},{1,5},{5... | collective-permute-start | bytes 1572872 | tf_op jit(solution)/shard_map/cond/branch_1_fun/ppermute | solution.py:190
  73.4 36.1 %collective-permute-start.19 = (bf16[2,512,512]{2,1,0:T(8,128)(2,1)S(1)}, bf16[2,512,512]{2,1,0:T(8,128)(2,1)}, u32[]{:S(2)}, u32[]{:S(2)}) collective-permute-start(bf16[2,512,512]{2,1,0:T(8,128)(2,1)S(1)} %collective-permute-done.14.rest_1_), channel_id=1, source_target_pairs={{0,1},{1,0},{2,3},{3,2},{4,5},{5,4},{6,7},{7,6},{8,9},{9,8},{10,11... | collective-permute-start | bytes 3145736 | tf_op jit(solution)/shard_map/cond/branch_1_fun/ppermute | solution.py:190
  74.0 35.5 %collective-permute-start.18 = (bf16[2,512,512]{2,1,0:T(8,128)(2,1)S(1)}, bf16[2,512,512]{2,1,0:T(8,128)(2,1)}, u32[]{:S(2)}, u32[]{:S(2)}) collective-permute-start(bf16[2,512,512]{2,1,0:T(8,128)(2,1)S(1)} %slice_bitcast_fusion.1.rest_0_), channel_id=1, source_target_pairs={{0,1},{1,0},{2,3},{3,2},{4,5},{5,4},{6,7},{7,6},{8,9},{9,8},{10,11... | collective-permute-start | bytes 3145736 | tf_op jit(solution)/shard_map/cond/branch_1_fun/ppermute | solution.py:190
  74.0 35.5 %collective-permute-start.20 = (bf16[2,512,512]{2,1,0:T(8,128)(2,1)S(1)}, bf16[2,512,512]{2,1,0:T(8,128)(2,1)}, u32[]{:S(2)}, u32[]{:S(2)}) collective-permute-start(bf16[2,512,512]{2,1,0:T(8,128)(2,1)S(1)} %collective-permute-done.15.rest_2_), channel_id=1, source_target_pairs={{0,1},{1,0},{2,3},{3,2},{4,5},{5,4},{6,7},{7,6},{8,9},{9,8},{10,11... | collective-permute-start | bytes 3145736 | tf_op jit(solution)/shard_map/cond/branch_1_fun/ppermute | solution.py:190
  107.2 2.3 collective-permute-start.23
  124.8 58.7 %all-to-all-start.7 = ((bf16[32,18,16,128]{3,2,1,0:T(8,128)(2,1)}), bf16[32,18,16,128]{3,2,1,0:T(8,128)(2,1)}, u32[]{:S(2)}, u32[]{:S(2)}) async-start(bf16[32,18,16,128]{3,2,1,0:T(8,128)(2,1)} %solve_0.6), calls=%async_computation.7 | async-start | bytes 4718592 | tf_op jit(solution)/shard_map/cond/branch_1_fun/all_to_all | solution.py:598
  131.7 32.7 %collective-permute-start.17 = (bf16[1,512,512]{2,1,0:T(8,128)(2,1)S(1)}, bf16[1,512,512]{2,1,0:T(8,128)(2,1)S(1)}, u32[]{:S(2)}, u32[]{:S(2)}) collective-permute-start(bf16[1,512,512]{2,1,0:T(8,128)(2,1)S(1)} %slice.34), channel_id=1, source_target_pairs={{0,2},{1,3},{2,0},{3,1},{4,6},{5,7},{6,4},{7,5},{8,10},{9,11},{10,... | collective-permute-start | bytes 1572872 | tf_op jit(solution)/shard_map/cond/branch_1_fun/ppermute | solution.py:190
  164.4 3.8 %collective-permute-start.21 = (bf16[1,512,512]{2,1,0:T(8,128)(2,1)S(1)}, bf16[1,512,512]{2,1,0:T(8,128)(2,1)S(1)}, u32[]{:S(2)}, u32[]{:S(2)}) collective-permute-start(bf16[1,512,512]{2,1,0:T(8,128)(2,1)S(1)} %collective-permute-done.17.rest_3_), channel_id=1, source_target_pairs={{0,1},{1,0},{2,3},{3,2},{4,5},{5,4},{6,7},{7,6},{8,9},{9,8},{10,11... | collective-permute-start | bytes 1572872 | tf_op jit(solution)/shard_map/cond/branch_1_fun/ppermute | solution.py:190
  183.4 58.7 %all-to-all-start.5 = ((bf16[32,18,16,128]{3,2,1,0:T(8,128)(2,1)}), bf16[32,18,16,128]{3,2,1,0:T(8,128)(2,1)S(1)}, u32[]{:S(2)}, u32[]{:S(2)}) async-start(bf16[32,18,16,128]{3,2,1,0:T(8,128)(2,1)} %solve_1.6), calls=%async_computation.5 | async-start | bytes 4718592 | tf_op jit(solution)/shard_map/cond/branch_1_fun/all_to_all | solution.py:598
  190.3 51.8 %copy-start.9 = (s32[544]{0:T(1024)S(1)}, s32[544]{0:T(1024)}, u32[]{:S(2)}) copy-start(s32[544]{0:T(1024)} %copy-done.8) | copy-start | bytes 6532 | tf_op jit(solution)/shard_map/cond
  194.4 54.2 %collective-permute-start.24 = (bf16[1,544,128]{2,1,0:T(8,128)(2,1)}, bf16[1,544,128]{2,1,0:T(8,128)(2,1)S(1)}, u32[]{:S(2)}, u32[]{:S(2)}) collective-permute-start(bf16[1,544,128]{2,1,0:T(8,128)(2,1)} %get-tuple-element.138), channel_id=1, source_target_pairs={{0,1},{1,2},{2,3},{3,4},{4,5},{5,6},{6,7},{7,8},{8,9},{9,10},{10,1... | collective-permute-start | bytes 417800 | tf_op jit(solution)/shard_map/cond/branch_1_fun/ppermute | solution.py:593
  197.7 50.9 %collective-permute-start.25 = (bf16[1,544,128]{2,1,0:T(8,128)(2,1)}, bf16[1,544,128]{2,1,0:T(8,128)(2,1)S(1)}, u32[]{:S(2)}, u32[]{:S(2)}) collective-permute-start(bf16[1,544,128]{2,1,0:T(8,128)(2,1)} %get-tuple-element.139), channel_id=1, source_target_pairs={{1,0},{2,1},{3,2},{4,3},{5,4},{6,5},{7,6},{8,7},{9,8},{10,9},{11,1... | collective-permute-start | bytes 417800 | tf_op jit(solution)/shard_map/cond/branch_1_fun/ppermute | solution.py:593
  243.6 8.8 %collective-permute-start.26 = (bf16[1,544,128]{2,1,0:T(8,128)(2,1)S(1)}, bf16[1,544,128]{2,1,0:T(8,128)(2,1)S(1)}, u32[]{:S(2)}, u32[]{:S(2)}) collective-permute-start(bf16[1,544,128]{2,1,0:T(8,128)(2,1)S(1)} %get-tuple-element.143), channel_id=1, source_target_pairs={{0,1},{1,2},{2,3},{3,4},{4,5},{5,6},{6,7},{7,8},{8,9},{9,10},{10,1... | collective-permute-start | bytes 417800 | tf_op jit(solution)/shard_map/cond/branch_1_fun/ppermute | solution.py:593
  246.7 8.2 %collective-permute-start.27 = (bf16[1,544,128]{2,1,0:T(8,128)(2,1)S(1)}, bf16[1,544,128]{2,1,0:T(8,128)(2,1)S(1)}, u32[]{:S(2)}, u32[]{:S(2)}) collective-permute-start(bf16[1,544,128]{2,1,0:T(8,128)(2,1)S(1)} %get-tuple-element.144), channel_id=1, source_target_pairs={{1,0},{2,1},{3,2},{4,3},{5,4},{6,5},{7,6},{8,7},{9,8},{10,9},{11,1... | collective-permute-start | bytes 417800 | tf_op jit(solution)/shard_map/cond/branch_1_fun/ppermute | solution.py:593
